TPU v7x, 256 devices: a whole 4x4x8 slice. The times are simulated.
256 devices in a mesh: gx: 8 (over y_lo, x), gy: 16 (over y_hi, z), gz: 2 (over core).
Axes of the slice: x: 4, y: 4 (y_hi: 2, y_lo: 2; y = y_hi * 2 + y_lo), z: 8, core: 2. Of those that a mesh axis runs over, the one named last changes fastest.
Arguments:
- surface_ids: int32 [256, 256, 256], P('gx', 'gy', 'gz'), may hold values from 0 to 256, as said below
- class_map: int32 [256, 256, 256], P('gx', 'gy', 'gz'), may hold values from 0 to 3
- conductivity: float32 [256, 256, 256], P('gx', 'gy', 'gz'), may hold values from 0.5 to 2
- normals: float32 [3, 256], replicated, may hold values from -9 to 9
- class_table: float32 [4], replicated, may hold values from 0.25 to 1
Outputs:
- distance: float32 [256, 256, 256], P('gx', 'gy', 'gz')
Inputs may be any that keep to these rules, and one draw needn't show every extreme that they name: `surface_ids`: 0 marks a cell without a source and k a cell of patch k; each cell holds a source with probability one quarter, of a patch drawn evenly.
All inputs are finite; a program needn't handle non-finite values.
Results may differ from a plain program's by a relative error of at most 0.0003.
Values sent between devices are 32-bit elements; how exact they have to be, the bound alone decides.
A program may use at most 128 MiB of HBM per device.

v0:
```python
import jax
import jax.numpy as jnp
from jax import lax
from jax.sharding import PartitionSpec as P

N = 256
STEPS = 8
RIM = 4
CLASSES = 4


time_step = 0.08
norm_floor = 0.5
offsets = ((1, 0, 0), (-1, 0, 0), (0, 1, 0), (0, -1, 0), (0, 0, 1), (0, 0, -1))


def padded_2(cells, sides, width):
    for axis, dim in sides:
        count = lax.axis_size(axis)
        ends = count - 1
        head = lax.slice_in_dim(cells, 0, width, axis=dim)
        tail = lax.slice_in_dim(cells, cells.shape[dim] - width, cells.shape[dim], axis=dim)
        cells = jnp.concatenate(
            [
                lax.ppermute(tail, axis, [(i, (i + 1) % count) for i in range(ends)]),
                cells,
                lax.ppermute(head, axis, [((i + 1) % count, i) for i in range(ends)]),
            ],
            axis=dim,
        )
    return cells


def shifted(padded, offset):
    extent = padded.shape[-3:]
    return padded[
        ...,
        1 + offset[0] : extent[0] - 1 + offset[0],
        1 + offset[1] : extent[1] - 1 + offset[1],
        1 + offset[2] : extent[2] - 1 + offset[2],
    ]


def diffuse(padded, root_field):
    center = shifted(padded, (0, 0, 0))
    middle = shifted(root_field, (0, 0, 0))
    inflow = jnp.zeros_like(center)
    for offset in offsets:
        inflow = inflow + shifted(root_field, offset) * (shifted(padded, offset) - center)
    return center + time_step * middle * inflow


def crop(values, crop_depth):
    if crop_depth == 0:
        return values
    return values[..., crop_depth:-crop_depth, crop_depth:-crop_depth, crop_depth:-crop_depth]


def cosine_table(length):
    wave_number = jnp.arange(length, dtype=jnp.float32)[:, None]
    sample = jnp.arange(length, dtype=jnp.float32)[None, :]
    factor = jnp.where(wave_number == 0, jnp.sqrt(1.0 / length), jnp.sqrt(2.0 / length))
    return factor * jnp.cos(jnp.pi * wave_number * (2.0 * sample + 1.0) / (2.0 * length))


def eigen_values(length):
    wave_number = jnp.arange(length, dtype=jnp.float32)
    return 2.0 - 2.0 * jnp.cos(jnp.pi * wave_number / length)


def normalize(heat_field):
    magnitude = jnp.sqrt(
        heat_field[0] * heat_field[0]
        + heat_field[1] * heat_field[1]
        + heat_field[2] * heat_field[2]
    )
    return heat_field / jnp.maximum(magnitude, norm_floor)


def along_last(values, matrix):
    return jnp.dot(values, matrix, precision=lax.Precision.HIGHEST)


def lookup_sources(surface_ids, lookup_table):
    cell_count = surface_ids.size
    block_cells = min(cell_count, 8192)
    block_count = cell_count // block_cells
    entries = lookup_table.shape[1]
    blocked_ids = surface_ids.reshape(block_count, block_cells)
    choices_row = jnp.arange(entries, dtype=jnp.int32)[None, :]

    def one_block(block_ids):
        one_hot = (block_ids[:, None] == choices_row).astype(jnp.float32)
        return jnp.einsum("ck,nk->cn", lookup_table, one_hot, precision=lax.Precision.HIGHEST)

    values = lax.map(one_block, blocked_ids)
    return values.transpose(1, 0, 2).reshape((3,) + surface_ids.shape)


def per_device(surface_ids, class_map, conductivity, normals, class_table):
    width_x, width_y, width_z = surface_ids.shape
    lookup_table = jnp.concatenate([jnp.zeros((3, 1), jnp.float32), normals], axis=1)
    source = lookup_sources(surface_ids, lookup_table)
    class_value = jnp.zeros(class_map.shape, jnp.float32)
    for class_index in range(CLASSES):
        class_value = class_value + jnp.where(
            class_map == class_index, class_table[class_index], 0.0
        )
    root_field = jnp.sqrt(class_value * conductivity)
    heat_field = source
    rim_root = padded_2(root_field, (("gx", 0), ("gy", 1), ("gz", 2)), RIM)
    for round_index in range(STEPS // RIM):
        padded = padded_2(heat_field, (("gx", 1), ("gy", 2), ("gz", 3)), RIM)
        for inner_step in range(RIM):
            padded = diffuse(padded, crop(rim_root, inner_step))
        heat_field = padded
    unit_field = normalize(heat_field)
    faces_x = padded_2(unit_field[0], (("gx", 0),), 1)
    faces_y = padded_2(unit_field[1], (("gy", 1),), 1)
    faces_z = padded_2(unit_field[2], (("gz", 2),), 1)
    part_x = 0.5 * (faces_x[2:] - faces_x[:-2])
    part_y = 0.5 * (faces_y[:, 2:] - faces_y[:, :-2])
    part_z = 0.5 * (faces_z[:, :, 2:] - faces_z[:, :, :-2])
    divergence = part_x + part_y + part_z
    cosine = cosine_table(N)
    forward = cosine.T
    narrow = lax.axis_size("gz")
    wide_count = lax.axis_size("gy")
    group_count = lax.axis_size("gx") * narrow
    x_rows = width_x // narrow
    kz_rows = N // wide_count
    ky_rows = N // group_count
    pencil = lax.all_to_all(divergence, "gz", split_axis=0, concat_axis=2, tiled=True)
    pencil = along_last(pencil.reshape(x_rows * width_y, N), forward)
    packed = (
        pencil.reshape(x_rows, width_y, wide_count, kz_rows)
        .transpose(2, 0, 1, 3)
        .reshape(wide_count, x_rows, width_y * kz_rows)
    )
    packed = lax.all_to_all(packed, "gy", split_axis=0, concat_axis=0, tiled=True)
    pencil = (
        packed.reshape(wide_count, x_rows, width_y, kz_rows)
        .transpose(1, 3, 0, 2)
        .reshape(x_rows * kz_rows, N)
    )
    pencil = along_last(pencil, forward)
    packed = (
        pencil.reshape(x_rows, kz_rows, group_count, ky_rows)
        .transpose(2, 0, 1, 3)
        .reshape(group_count, x_rows, kz_rows * ky_rows)
    )
    packed = lax.all_to_all(packed, ("gx", "gz"), split_axis=0, concat_axis=0, tiled=True)
    pencil = (
        packed.reshape(group_count, x_rows, kz_rows, ky_rows)
        .transpose(2, 3, 0, 1)
        .reshape(kz_rows * ky_rows, N)
    )
    pencil = along_last(pencil, forward)
    spectra = eigen_values(N)
    group_index = lax.axis_index("gx") * narrow + lax.axis_index("gz")
    spectra_z = lax.dynamic_slice_in_dim(spectra, lax.axis_index("gy") * kz_rows, kz_rows)
    spectra_y = lax.dynamic_slice_in_dim(spectra, group_index * ky_rows, ky_rows)
    screen = 4.0 / (N * N)
    divisor = spectra[None, None, :] + spectra_y[None, :, None] + spectra_z[:, None, None] + screen
    pencil = -pencil / divisor.reshape(kz_rows * ky_rows, N)
    pencil = along_last(pencil, cosine)
    packed = (
        pencil.reshape(kz_rows, ky_rows, group_count, x_rows)
        .transpose(2, 3, 0, 1)
        .reshape(group_count, x_rows, kz_rows * ky_rows)
    )
    packed = lax.all_to_all(packed, ("gx", "gz"), split_axis=0, concat_axis=0, tiled=True)
    pencil = (
        packed.reshape(group_count, x_rows, kz_rows, ky_rows)
        .transpose(1, 2, 0, 3)
        .reshape(x_rows * kz_rows, N)
    )
    pencil = along_last(pencil, cosine)
    packed = (
        pencil.reshape(x_rows, kz_rows, wide_count, width_y)
        .transpose(2, 0, 3, 1)
        .reshape(wide_count, x_rows, width_y * kz_rows)
    )
    packed = lax.all_to_all(packed, "gy", split_axis=0, concat_axis=0, tiled=True)
    pencil = (
        packed.reshape(wide_count, x_rows, width_y, kz_rows)
        .transpose(1, 2, 0, 3)
        .reshape(x_rows * width_y, N)
    )
    pencil = along_last(pencil, cosine).reshape(x_rows, width_y, N)
    return lax.all_to_all(pencil, "gz", split_axis=2, concat_axis=0, tiled=True)


def solution(mesh):
    in_specs = (P("gx", "gy", "gz"), P("gx", "gy", "gz"), P("gx", "gy", "gz"), P(), P())
    out_specs = P("gx", "gy", "gz")
    return jax.shard_map(
        per_device, mesh=mesh, in_specs=in_specs, out_specs=out_specs, check_vma=False
    )
```

profile of v0, /device:TPU:1, one launch (start us, length us, event | category | flops | bytes accessed | tf_op | source)
XLA Modules:
  0.0 351.5 jit_solution(15492658325583799852)
XLA Ops:
  1.5 4.4 %broadcast_multiply_fusion = (f32[32,16,128]{2,1,0:T(8,128)}, f32[32,16,128]{2,1,0:T(8,128)S(1)}) fusion(f32[32,16,128]{2,1,0:T(8,128)} %param.9, f32[]{:T(128)} %bitcast.4, s32[32,16,128]{2,1,0:T(8,128)} %param.8, f32[]{:T(128)} %bitcast.3, f32[]{:T(128)} %bitcast.2, f32[]{:T(128)} %bitcast.1), kind=kLoop, calls=%fused_computation.253 | loop fusion | flops 851968 | bytes 1048592 | tf_op jit(solution)/shard_map/mul | solution.py:50
  5.9 3.9 %collective-permute-start.6 = (f32[4,16,128]{2,1,0:T(8,128)S(1)}, f32[4,16,128]{2,1,0:T(8,128)S(1)}, u32[]{:S(2)}, u32[]{:S(2)}) collective-permute-start(f32[4,16,128]{2,1,0:T(8,128)S(1)} %get-tuple-element.105), channel_id=1, source_target_pairs={{0,32},{32,64},{64,96},{96,128},{128,160},{160,192},{192,224},{1,3... | collective-permute-start | bytes 98312 | tf_op jit(solution)/shard_map/ppermute | solution.py:25
  12.9 28.2 %while.11 = (s32[]{:T(128)}, f32[8,3,8192]{2,1,0:T(4,128)}, s32[8,8192]{1,0:T(8,128)S(1)}, f32[3,257]{1,0:T(4,128)S(1)}, s32[]{:T(128)}) while((s32[]{:T(128)}, f32[8,3,8192]{2,1,0:T(4,128)}, s32[8,8192]{1,0:T(8,128)S(1)}, f32[3,257]{1,0:T(4,128)S(1)}, s32[]{:T(128)}) %tuple.63), condition=%wide.region_1.2_spmd.clone, body=%wide.region_0.1_spmd.clone.sunk | while | flops 77897728 | bytes 233037 | solution.py:96
  42.9 4.0 %collective-permute-start = (f32[3,4,16,128]{3,2,1,0:T(8,128)S(1)}, f32[3,4,16,128]{3,2,1,0:T(8,128)S(1)}, u32[]{:S(2)}, u32[]{:S(2)}) collective-permute-start(f32[3,4,16,128]{3,2,1,0:T(8,128)S(1)} %get-tuple-element.88), channel_id=1, source_target_pairs={{0,32},{32,64},{64,96},{96,128},{128,160},{160,192},{192,224},{1,3... | collective-permute-start | bytes 294920 | tf_op jit(solution)/shard_map/ppermute | solution.py:25
  53.3 4.2 %collective-permute-start.2 = (f32[3,40,4,128]{3,2,1,0:T(4,128)S(1)}, f32[3,40,4,128]{3,2,1,0:T(4,128)S(1)}, u32[]{:S(2)}, u32[]{:S(2)}) collective-permute-start(f32[3,40,4,128]{3,2,1,0:T(4,128)S(1)} %get-tuple-element.78), channel_id=1, source_target_pairs={{0,2},{2,4},{4,6},{6,8},{8,10},{10,12},{12,14},{14,16},{16,18},{18... | collective-permute-start | bytes 737288 | tf_op jit(solution)/shard_map/ppermute | solution.py:25
  60.4 4.1 %collective-permute-start.11 = (f32[40,24,4]{2,1,0:T(8,128)S(1)}, f32[40,24,4]{2,1,0:T(8,128)S(1)}, u32[]{:S(2)}, u32[]{:S(2)}) collective-permute-start(f32[40,24,4]{2,1,0:T(8,128)S(1)} %get-tuple-element.94), channel_id=1, source_target_pairs={{1,0},{3,2},{5,4},{7,6},{9,8},{11,10},{13,12},{15,14},{17,16},{19,... | collective-permute-start | bytes 46088 | tf_op jit(solution)/shard_map/ppermute | solution.py:27
  70.3 4.0 %slice_multiply_fusion.1 = (f32[36,20,132]{2,1,0:T(8,128)S(1)}, f32[36,20,132]{2,1,0:T(8,128)}, f32[36,20,132]{2,1,0:T(8,128)}, f32[36,20,132]{2,1,0:T(8,128)}, ...) fusion(f32[40,24,136]{2,1,0:T(8,128)S(1)} %pad_maximum_fusion.4), kind=kLoop, calls=%fused_computation.133 | loop fusion | flops 95040 | bytes 5322240 | tf_op jit(solution)/shard_map/mul | solution.py:50
  88.0 4.7 %collective-permute-start.5 = (f32[3,40,24,4]{1,2,3,0:T(8,128)}, f32[3,40,24,4]{1,2,3,0:T(8,128)}, u32[]{:S(2)}, u32[]{:S(2)}) collective-permute-start(f32[3,40,24,4]{1,2,3,0:T(8,128)} %copy.39), channel_id=1, source_target_pairs={{1,0},{3,2},{5,4},{7,6},{9,8},{11,10},{13,12},{15,14},{17,16},{19,... | collective-permute-start | bytes 138248 | tf_op jit(solution)/shard_map/ppermute | solution.py:27
  102.5 4.0 %pad_maximum_fusion = f32[3,40,24,136]{3,2,1,0:T(8,128)S(1)} fusion(f32[3,40,24,4]{3,2,1,0:T(8,128)} %copy.41, f32[3,40,4,128]{3,2,1,0:T(4,128)S(1)} %copy-done.61, f32[3,40,16,128]{3,2,1,0:T(8,128)} %copy-done.36, f32[3,40,4,128]{3,2,1,0:T(4,128)S(1)} %copy-done.59, f32[3,40,24,4]{3,2,1,0:T(8,128)} %copy.40), kind=kLoop, calls=%fused_computation.6 | loop fusion | flops 1566720 | bytes 3133440 | tf_op jit(solution)/shard_map/concatenate | solution.py:23
  106.7 4.7 %fusion.20 = f32[3,38,22,134]{3,2,1,0:T(8,128)S(1)} fusion(f32[3,40,24,136]{3,2,1,0:T(8,128)S(1)} %pad_maximum_fusion, f32[38,22,134]{2,1,0:T(8,128)S(1)} %get-tuple-element.72, f32[38,22,134]{2,1,0:T(8,128)S(1)} %copy-done, f32[38,22,134]{2,1,0:T(8,128)S(1)} %copy-done.2, f32[38,22,134]{2,1,0:T(8,128)S(1)} %copy-done.4, f32[38,22,134]{2,1,0:T(8,128)S(1)} %copy-done.6, ...), kind=kLoop, calls=%fused_computation.31 | loop fusion | flops 6385368 | bytes 13890976 | tf_op jit(solution)/shard_map/add | solution.py:50
  111.5 4.5 %fusion.46 = f32[3,36,20,132]{3,2,1,0:T(8,128)S(1)} fusion(f32[3,38,22,134]{3,2,1,0:T(8,128)S(1)} %fusion.20, f32[36,20,132]{2,1,0:T(8,128)S(1)} %copy-done.10, f32[36,20,132]{2,1,0:T(8,128)S(1)} %copy-done.12, f32[36,20,132]{2,1,0:T(8,128)S(1)} %copy-done.14, f32[36,20,132]{2,1,0:T(8,128)S(1)} %copy-done.16, f32[36,20,132]{2,1,0:T(8,128)S(1)} %copy-done.18, ...), kind=kLoop, calls=%fused_computation.69 | loop fusion | flops 5417280 | bytes 11784960 | tf_op jit(solution)/shard_map/add | solution.py:50
  116.1 4.2 %fusion.72 = f32[3,34,18,130]{3,2,1,0:T(8,128)S(1)} fusion(f32[3,36,20,132]{3,2,1,0:T(8,128)S(1)} %fusion.46, f32[34,18,130]{2,1,0:T(8,128)S(1)} %copy-done.24, f32[34,18,130]{2,1,0:T(8,128)S(1)} %copy-done.22, f32[34,18,130]{2,1,0:T(8,128)S(1)} %copy-done.28, f32[34,18,130]{2,1,0:T(8,128)S(1)} %copy-done.30, f32[34,18,130]{2,1,0:T(8,128)S(1)} %copy-done.32, ...), kind=kLoop, calls=%fused_computation.107 | loop fusion | flops 4534920 | bytes 9865440 | tf_op jit(solution)/shard_map/add | solution.py:50
  121.7 4.3 %collective-permute-start.12 = (f32[3,4,16,128]{3,2,1,0:T(8,128)S(1)}, f32[3,4,16,128]{3,2,1,0:T(8,128)S(1)}, u32[]{:S(2)}, u32[]{:S(2)}) collective-permute-start(f32[3,4,16,128]{3,2,1,0:T(8,128)S(1)} %get-tuple-element.85), channel_id=1, source_target_pairs={{0,32},{32,64},{64,96},{96,128},{128,160},{160,192},{192,224},{1,3... | collective-permute-start | bytes 294920 | tf_op jit(solution)/shard_map/ppermute | solution.py:25
  127.8 4.1 %collective-permute-done.13 = f32[3,4,16,128]{3,2,1,0:T(8,128)S(1)} collective-permute-done((f32[3,4,16,128]{3,2,1,0:T(8,128)S(1)}, f32[3,4,16,128]{3,2,1,0:T(8,128)S(1)}, u32[]{:S(2)}, u32[]{:S(2)}) %collective-permute-start.13) | collective-permute-done | bytes 98336 | tf_op jit(solution)/shard_map/ppermute | solution.py:27
  132.0 15.1 %collective-permute-start.14 = (f32[3,40,4,128]{3,2,1,0:T(4,128)S(1)}, f32[3,40,4,128]{3,2,1,0:T(4,128)S(1)}, u32[]{:S(2)}, u32[]{:S(2)}) collective-permute-start(f32[3,40,4,128]{3,2,1,0:T(4,128)S(1)} %get-tuple-element.57), channel_id=1, source_target_pairs={{0,2},{2,4},{4,6},{6,8},{8,10},{10,12},{12,14},{14,16},{16,18},{18... | collective-permute-start | bytes 737288 | tf_op jit(solution)/shard_map/ppermute | solution.py:25
  152.2 5.3 %collective-permute-done.15 = f32[3,40,4,128]{3,2,1,0:T(4,128)S(1)} collective-permute-done((f32[3,40,4,128]{3,2,1,0:T(4,128)S(1)}, f32[3,40,4,128]{3,2,1,0:T(4,128)S(1)}, u32[]{:S(2)}, u32[]{:S(2)}) %collective-permute-start.15) | collective-permute-done | bytes 245792 | tf_op jit(solution)/shard_map/ppermute | solution.py:27
  167.0 4.3 %collective-permute-start.17 = (f32[3,40,24,4]{1,2,3,0:T(8,128)}, f32[3,40,24,4]{1,2,3,0:T(8,128)}, u32[]{:S(2)}, u32[]{:S(2)}) collective-permute-start(f32[3,40,24,4]{1,2,3,0:T(8,128)} %copy.43), channel_id=1, source_target_pairs={{1,0},{3,2},{5,4},{7,6},{9,8},{11,10},{13,12},{15,14},{17,16},{19,... | collective-permute-start | bytes 138248 | tf_op jit(solution)/shard_map/ppermute | solution.py:27
  176.6 4.0 %pad_maximum_fusion.1 = f32[3,40,24,136]{3,2,1,0:T(8,128)S(1)} fusion(f32[3,40,24,4]{3,2,1,0:T(8,128)} %copy.45, f32[3,40,4,128]{3,2,1,0:T(4,128)} %copy-done.63, f32[3,4,16,128]{3,2,1,0:T(8,128)} %copy-done.65, f32[3,32,16,128]{3,2,1,0:T(8,128)S(1)} %fusion.99, f32[3,4,16,128]{3,2,1,0:T(8,128)} %copy-done.64, f32[3,40,4,128]{3,2,1,0:T(4,128)} %copy-done.62, ...), kind=kLoop, calls=%fused_computation.7 | loop fusion | flops 2350080 | bytes 3133440 | tf_op jit(solution)/shard_map/concatenate | solution.py:23
  180.6 4.7 %fusion.7 = f32[3,38,22,134]{3,2,1,0:T(8,128)S(1)} fusion(f32[3,40,24,136]{3,2,1,0:T(8,128)S(1)} %pad_maximum_fusion.1, f32[38,22,134]{2,1,0:T(8,128)S(1)} %get-tuple-element.72, f32[38,22,134]{2,1,0:T(8,128)S(1)} %copy-done.1, f32[38,22,134]{2,1,0:T(8,128)S(1)} %copy-done.3, f32[38,22,134]{2,1,0:T(8,128)S(1)} %copy-done.5, f32[38,22,134]{2,1,0:T(8,128)S(1)} %copy-done.7, ...), kind=kLoop, calls=%fused_computation.12 | loop fusion | flops 6385368 | bytes 13890976 | tf_op jit(solution)/shard_map/add | solution.py:50
  185.4 4.5 %fusion.33 = f32[3,36,20,132]{3,2,1,0:T(8,128)S(1)} fusion(f32[3,38,22,134]{3,2,1,0:T(8,128)S(1)} %fusion.7, f32[36,20,132]{2,1,0:T(8,128)S(1)} %copy-done.11, f32[36,20,132]{2,1,0:T(8,128)S(1)} %copy-done.13, f32[36,20,132]{2,1,0:T(8,128)S(1)} %copy-done.15, f32[36,20,132]{2,1,0:T(8,128)S(1)} %copy-done.17, f32[36,20,132]{2,1,0:T(8,128)S(1)} %copy-done.19, ...), kind=kLoop, calls=%fused_computation.50 | loop fusion | flops 5417280 | bytes 11784960 | tf_op jit(solution)/shard_map/add | solution.py:50
  190.1 4.2 %fusion.59 = f32[3,34,18,130]{3,2,1,0:T(8,128)S(1)} fusion(f32[3,36,20,132]{3,2,1,0:T(8,128)S(1)} %fusion.33, f32[34,18,130]{2,1,0:T(8,128)S(1)} %copy-done.25, f32[34,18,130]{2,1,0:T(8,128)S(1)} %copy-done.23, f32[34,18,130]{2,1,0:T(8,128)S(1)} %copy-done.29, f32[34,18,130]{2,1,0:T(8,128)S(1)} %copy-done.31, f32[34,18,130]{2,1,0:T(8,128)S(1)} %copy-done.33, ...), kind=kLoop, calls=%fused_computation.88 | loop fusion | flops 4534920 | bytes 9865440 | tf_op jit(solution)/shard_map/add | solution.py:50
  201.2 5.5 %collective-permute-start.21 = (f32[32,1,128]{2,1,0:T(1,128)S(1)}, f32[32,1,128]{2,1,0:T(1,128)S(1)}, u32[]{:S(2)}, u32[]{:S(2)}) collective-permute-start(f32[32,1,128]{2,1,0:T(1,128)S(1)} %get-tuple-element.102), channel_id=1, source_target_pairs={{0,2},{2,4},{4,6},{6,8},{8,10},{10,12},{12,14},{14,16},{16,18},{18... | collective-permute-start | bytes 49160 | tf_op jit(solution)/shard_map/ppermute | solution.py:25
  208.0 4.9 %collective-permute-start.19 = (f32[1,16,128]{2,1,0:T(8,128)S(1)}, f32[1,16,128]{2,1,0:T(8,128)S(1)}, u32[]{:S(2)}, u32[]{:S(2)}) collective-permute-start(f32[1,16,128]{2,1,0:T(8,128)S(1)} %get-tuple-element.81), channel_id=1, source_target_pairs={{0,32},{32,64},{64,96},{96,128},{128,160},{160,192},{192,224},{1,3... | collective-permute-start | bytes 24584 | tf_op jit(solution)/shard_map/ppermute | solution.py:25
  214.0 6.0 %all_to_all.53 = f32[32,16,128]{2,1,0:T(8,128)S(1)} all-to-all(f32[32,16,128]{2,1,0:T(8,128)S(1)} %fusion.111), channel_id=1, replica_groups=mesh['gx'=8,'gy'=16,'gz'=2] {'gz'}, dimensions={0} | all-to-all | bytes 524288 | tf_op jit(solution)/shard_map/all_to_all | solution.py:133
  224.9 16.8 %all-to-all-start.1 = ((f32[16,16,256]{2,1,0:T(8,128)}), f32[16,16,256]{2,1,0:T(8,128)S(1)}, u32[]{:S(2)}, u32[]{:S(2)}) async-start(f32[16,16,256]{2,1,0:T(8,128)} %copy.47), calls=%async_computation.1 | async-start | bytes 524288 | tf_op jit(solution)/shard_map/all_to_all | solution.py:140
  242.0 10.2 %all-to-all-done.1 = f32[16,16,256]{2,1,0:T(8,128)S(1)} async-done(((f32[16,16,256]{2,1,0:T(8,128)}), f32[16,16,256]{2,1,0:T(8,128)S(1)}, u32[]{:S(2)}, u32[]{:S(2)}) %all-to-all-start.1) | async-done | bytes 262176 | tf_op jit(solution)/shard_map/all_to_all | solution.py:140
  261.6 17.1 %all-to-all-start.2 = ((f32[16,16,256]{2,1,0:T(8,128)}), f32[16,16,256]{2,1,0:T(8,128)S(1)}, u32[]{:S(2)}, u32[]{:S(2)}) async-start(f32[16,16,256]{2,1,0:T(8,128)} %copy.49), calls=%async_computation.2 | async-start | bytes 524288 | tf_op jit(solution)/shard_map/all_to_all | solution.py:152
  278.9 6.9 %all-to-all-done.2 = f32[16,16,256]{2,1,0:T(8,128)S(1)} async-done(((f32[16,16,256]{2,1,0:T(8,128)}), f32[16,16,256]{2,1,0:T(8,128)S(1)}, u32[]{:S(2)}, u32[]{:S(2)}) %all-to-all-start.2) | async-done | bytes 262176 | tf_op jit(solution)/shard_map/all_to_all | solution.py:152
  293.1 4.4 %all-to-all-start.3 = ((f32[16,16,256]{2,1,0:T(8,128)}), f32[16,16,256]{2,1,0:T(8,128)S(1)}, u32[]{:S(2)}, u32[]{:S(2)}) async-start(f32[16,16,256]{2,1,0:T(8,128)} %copy.61), calls=%async_computation.3 | async-start | bytes 524288 | tf_op jit(solution)/shard_map/all_to_all | solution.py:172
  297.5 7.1 %all-to-all-done.3 = f32[16,16,256]{2,1,0:T(8,128)S(1)} async-done(((f32[16,16,256]{2,1,0:T(8,128)}), f32[16,16,256]{2,1,0:T(8,128)S(1)}, u32[]{:S(2)}, u32[]{:S(2)}) %all-to-all-start.3) | async-done | bytes 262176 | tf_op jit(solution)/shard_map/all_to_all | solution.py:172
  317.1 14.1 %all_to_all.54 = f32[16,16,256]{2,1,0:T(8,128)S(1)} all-to-all(f32[16,16,256]{2,1,0:T(8,128)S(1)} %reshape.220), channel_id=1, replica_groups=mesh['gx'=8,'gy'=16,'gz'=2] {'gy'}, dimensions={0} | all-to-all | bytes 524288 | tf_op jit(solution)/shard_map/all_to_all | solution.py:184
  340.4 6.7 %all_to_all.55 = f32[2,1,32768]{2,1,0:T(1,128)S(1)} all-to-all(f32[2,1,32768]{2,1,0:T(1,128)S(1)} %reshape.231), channel_id=1, replica_groups=mesh['gx'=8,'gy'=16,'gz'=2] {'gz'}, dimensions={0} | all-to-all | bytes 524288 | tf_op jit(solution)/shard_map/all_to_all | solution.py:191
  (273 shorter events, 152.8 us)
Async XLA Ops:
  5.9 42.3 %collective-permute-start.6 = (f32[4,16,128]{2,1,0:T(8,128)S(1)}, f32[4,16,128]{2,1,0:T(8,128)S(1)}, u32[]{:S(2)}, u32[]{:S(2)}) collective-permute-start(f32[4,16,128]{2,1,0:T(8,128)S(1)} %get-tuple-element.105), channel_id=1, source_target_pairs={{0,32},{32,64},{64,96},{96,128},{128,160},{160,192},{192,224},{1,3... | collective-permute-start | bytes 98312 | tf_op jit(solution)/shard_map/ppermute | solution.py:25
  9.8 38.4 %collective-permute-start.7 = (f32[4,16,128]{2,1,0:T(8,128)S(1)}, f32[4,16,128]{2,1,0:T(8,128)S(1)}, u32[]{:S(2)}, u32[]{:S(2)}) collective-permute-start(f32[4,16,128]{2,1,0:T(8,128)S(1)} %get-tuple-element.106), channel_id=1, source_target_pairs={{32,0},{64,32},{96,64},{128,96},{160,128},{192,160},{224,192},{33,... | collective-permute-start | bytes 98312 | tf_op jit(solution)/shard_map/ppermute | solution.py:27
  42.9 10.2 %collective-permute-start = (f32[3,4,16,128]{3,2,1,0:T(8,128)S(1)}, f32[3,4,16,128]{3,2,1,0:T(8,128)S(1)}, u32[]{:S(2)}, u32[]{:S(2)}) collective-permute-start(f32[3,4,16,128]{3,2,1,0:T(8,128)S(1)} %get-tuple-element.88), channel_id=1, source_target_pairs={{0,32},{32,64},{64,96},{96,128},{128,160},{160,192},{192,224},{1,3... | collective-permute-start | bytes 294920 | tf_op jit(solution)/shard_map/ppermute | solution.py:25
  46.9 6.3 %collective-permute-start.1 = (f32[3,4,16,128]{3,2,1,0:T(8,128)S(1)}, f32[3,4,16,128]{3,2,1,0:T(8,128)S(1)}, u32[]{:S(2)}, u32[]{:S(2)}) collective-permute-start(f32[3,4,16,128]{3,2,1,0:T(8,128)S(1)} %get-tuple-element.87), channel_id=1, source_target_pairs={{32,0},{64,32},{96,64},{128,96},{160,128},{192,160},{224,192},{33,... | collective-permute-start | bytes 294920 | tf_op jit(solution)/shard_map/ppermute | solution.py:27
  48.3 10.6 %collective-permute-start.8 = (f32[40,4,128]{2,1,0:T(4,128)S(1)}, f32[40,4,128]{2,1,0:T(4,128)S(1)}, u32[]{:S(2)}, u32[]{:S(2)}) collective-permute-start(f32[40,4,128]{2,1,0:T(4,128)S(1)} %get-tuple-element.96), channel_id=1, source_target_pairs={{0,2},{2,4},{4,6},{6,8},{8,10},{10,12},{12,14},{14,16},{16,18},{18... | collective-permute-start | bytes 245768 | tf_op jit(solution)/shard_map/ppermute | solution.py:25
  51.8 7.0 %collective-permute-start.9 = (f32[40,4,128]{2,1,0:T(4,128)S(1)}, f32[40,4,128]{2,1,0:T(4,128)S(1)}, u32[]{:S(2)}, u32[]{:S(2)}) collective-permute-start(f32[40,4,128]{2,1,0:T(4,128)S(1)} %get-tuple-element.97), channel_id=1, source_target_pairs={{2,0},{4,2},{6,4},{8,6},{10,8},{12,10},{14,12},{16,14},{18,16},{20... | collective-permute-start | bytes 245768 | tf_op jit(solution)/shard_map/ppermute | solution.py:27
  53.2 26.0 %copy-start.36 = (f32[3,40,16,128]{3,2,1,0:T(8,128)}, f32[3,40,16,128]{3,2,1,0:T(8,128)S(1)}, u32[]{:S(2)}) copy-start(f32[3,40,16,128]{3,2,1,0:T(8,128)S(1)} %constant_dynamic-update-slice_fusion) | copy-start | bytes 2949124
  53.3 25.9 %collective-permute-start.2 = (f32[3,40,4,128]{3,2,1,0:T(4,128)S(1)}, f32[3,40,4,128]{3,2,1,0:T(4,128)S(1)}, u32[]{:S(2)}, u32[]{:S(2)}) collective-permute-start(f32[3,40,4,128]{3,2,1,0:T(4,128)S(1)} %get-tuple-element.78), channel_id=1, source_target_pairs={{0,2},{2,4},{4,6},{6,8},{8,10},{10,12},{12,14},{14,16},{16,18},{18... | collective-permute-start | bytes 737288 | tf_op jit(solution)/shard_map/ppermute | solution.py:25
  57.5 21.7 %collective-permute-start.3 = (f32[3,40,4,128]{3,2,1,0:T(4,128)S(1)}, f32[3,40,4,128]{3,2,1,0:T(4,128)S(1)}, u32[]{:S(2)}, u32[]{:S(2)}) collective-permute-start(f32[3,40,4,128]{3,2,1,0:T(4,128)S(1)} %get-tuple-element.79), channel_id=1, source_target_pairs={{2,0},{4,2},{6,4},{8,6},{10,8},{12,10},{14,12},{16,14},{18,16},{20... | collective-permute-start | bytes 737288 | tf_op jit(solution)/shard_map/ppermute | solution.py:27
  58.8 18.6 %copy-start.54 = (f32[40,4,128]{2,1,0:T(4,128)}, f32[40,4,128]{2,1,0:T(4,128)S(1)}, u32[]{:S(2)}) copy-start(f32[40,4,128]{2,1,0:T(4,128)S(1)} %collective-permute-done.8) | copy-start | bytes 245764
  58.9 18.5 %copy-start.55 = (f32[40,4,128]{2,1,0:T(4,128)}, f32[40,4,128]{2,1,0:T(4,128)S(1)}, u32[]{:S(2)}) copy-start(f32[40,4,128]{2,1,0:T(4,128)S(1)} %collective-permute-done.9) | copy-start | bytes 245764
  59.1 6.4 %collective-permute-start.10 = (f32[40,24,4]{2,1,0:T(8,128)S(1)}, f32[40,24,4]{2,1,0:T(8,128)S(1)}, u32[]{:S(2)}, u32[]{:S(2)}) collective-permute-start(f32[40,24,4]{2,1,0:T(8,128)S(1)} %get-tuple-element.93), channel_id=1, source_target_pairs={{0,1},{2,3},{4,5},{6,7},{8,9},{10,11},{12,13},{14,15},{16,17},{18,... | collective-permute-start | bytes 46088 | tf_op jit(solution)/shard_map/ppermute | solution.py:25
  60.4 5.6 %collective-permute-start.11 = (f32[40,24,4]{2,1,0:T(8,128)S(1)}, f32[40,24,4]{2,1,0:T(8,128)S(1)}, u32[]{:S(2)}, u32[]{:S(2)}) collective-permute-start(f32[40,24,4]{2,1,0:T(8,128)S(1)} %get-tuple-element.94), channel_id=1, source_target_pairs={{1,0},{3,2},{5,4},{7,6},{9,8},{11,10},{13,12},{15,14},{17,16},{19,... | collective-permute-start | bytes 46088 | tf_op jit(solution)/shard_map/ppermute | solution.py:27
  84.1 13.1 %collective-permute-start.4 = (f32[3,40,24,4]{1,2,3,0:T(8,128)}, f32[3,40,24,4]{1,2,3,0:T(8,128)}, u32[]{:S(2)}, u32[]{:S(2)}) collective-permute-start(f32[3,40,24,4]{1,2,3,0:T(8,128)} %copy.38), channel_id=1, source_target_pairs={{0,1},{2,3},{4,5},{6,7},{8,9},{10,11},{12,13},{14,15},{16,17},{18,... | collective-permute-start | bytes 138248 | tf_op jit(solution)/shard_map/ppermute | solution.py:25
  88.0 11.8 %collective-permute-start.5 = (f32[3,40,24,4]{1,2,3,0:T(8,128)}, f32[3,40,24,4]{1,2,3,0:T(8,128)}, u32[]{:S(2)}, u32[]{:S(2)}) collective-permute-start(f32[3,40,24,4]{1,2,3,0:T(8,128)} %copy.39), channel_id=1, source_target_pairs={{1,0},{3,2},{5,4},{7,6},{9,8},{11,10},{13,12},{15,14},{17,16},{19,... | collective-permute-start | bytes 138248 | tf_op jit(solution)/shard_map/ppermute | solution.py:27
  121.7 6.1 %collective-permute-start.12 = (f32[3,4,16,128]{3,2,1,0:T(8,128)S(1)}, f32[3,4,16,128]{3,2,1,0:T(8,128)S(1)}, u32[]{:S(2)}, u32[]{:S(2)}) collective-permute-start(f32[3,4,16,128]{3,2,1,0:T(8,128)S(1)} %get-tuple-element.85), channel_id=1, source_target_pairs={{0,32},{32,64},{64,96},{96,128},{128,160},{160,192},{192,224},{1,3... | collective-permute-start | bytes 294920 | tf_op jit(solution)/shard_map/ppermute | solution.py:25
  126.0 5.9 %collective-permute-start.13 = (f32[3,4,16,128]{3,2,1,0:T(8,128)S(1)}, f32[3,4,16,128]{3,2,1,0:T(8,128)S(1)}, u32[]{:S(2)}, u32[]{:S(2)}) collective-permute-start(f32[3,4,16,128]{3,2,1,0:T(8,128)S(1)} %get-tuple-element.86), channel_id=1, source_target_pairs={{32,0},{64,32},{96,64},{128,96},{160,128},{192,160},{224,192},{33,... | collective-permute-start | bytes 294920 | tf_op jit(solution)/shard_map/ppermute | solution.py:27
  127.8 29.6 %copy-start.64 = (f32[3,4,16,128]{3,2,1,0:T(8,128)}, f32[3,4,16,128]{3,2,1,0:T(8,128)S(1)}, u32[]{:S(2)}) copy-start(f32[3,4,16,128]{3,2,1,0:T(8,128)S(1)} %collective-permute-done.12) | copy-start | bytes 294916
  131.9 25.5 %copy-start.65 = (f32[3,4,16,128]{3,2,1,0:T(8,128)}, f32[3,4,16,128]{3,2,1,0:T(8,128)S(1)}, u32[]{:S(2)}) copy-start(f32[3,4,16,128]{3,2,1,0:T(8,128)S(1)} %collective-permute-done.13) | copy-start | bytes 294916
  132.0 20.1 %collective-permute-start.14 = (f32[3,40,4,128]{3,2,1,0:T(4,128)S(1)}, f32[3,40,4,128]{3,2,1,0:T(4,128)S(1)}, u32[]{:S(2)}, u32[]{:S(2)}) collective-permute-start(f32[3,40,4,128]{3,2,1,0:T(4,128)S(1)} %get-tuple-element.57), channel_id=1, source_target_pairs={{0,2},{2,4},{4,6},{6,8},{8,10},{10,12},{12,14},{14,16},{16,18},{18... | collective-permute-start | bytes 737288 | tf_op jit(solution)/shard_map/ppermute | solution.py:25
  147.1 10.4 %collective-permute-start.15 = (f32[3,40,4,128]{3,2,1,0:T(4,128)S(1)}, f32[3,40,4,128]{3,2,1,0:T(4,128)S(1)}, u32[]{:S(2)}, u32[]{:S(2)}) collective-permute-start(f32[3,40,4,128]{3,2,1,0:T(4,128)S(1)} %get-tuple-element.58), channel_id=1, source_target_pairs={{2,0},{4,2},{6,4},{8,6},{10,8},{12,10},{14,12},{16,14},{18,16},{20... | collective-permute-start | bytes 737288 | tf_op jit(solution)/shard_map/ppermute | solution.py:27
  163.1 8.2 %collective-permute-start.16 = (f32[3,40,24,4]{1,2,3,0:T(8,128)}, f32[3,40,24,4]{1,2,3,0:T(8,128)}, u32[]{:S(2)}, u32[]{:S(2)}) collective-permute-start(f32[3,40,24,4]{1,2,3,0:T(8,128)} %copy.42), channel_id=1, source_target_pairs={{0,1},{2,3},{4,5},{6,7},{8,9},{10,11},{12,13},{14,15},{16,17},{18,... | collective-permute-start | bytes 138248 | tf_op jit(solution)/shard_map/ppermute | solution.py:25
  167.0 7.0 %collective-permute-start.17 = (f32[3,40,24,4]{1,2,3,0:T(8,128)}, f32[3,40,24,4]{1,2,3,0:T(8,128)}, u32[]{:S(2)}, u32[]{:S(2)}) collective-permute-start(f32[3,40,24,4]{1,2,3,0:T(8,128)} %copy.43), channel_id=1, source_target_pairs={{1,0},{3,2},{5,4},{7,6},{9,8},{11,10},{13,12},{15,14},{17,16},{19,... | collective-permute-start | bytes 138248 | tf_op jit(solution)/shard_map/ppermute | solution.py:27
  197.3 10.7 %collective-permute-start.22 = (f32[32,16,1]{2,1,0:T(8,128)S(1)}, f32[32,16,1]{2,1,0:T(8,128)S(1)}, u32[]{:S(2)}, u32[]{:S(2)}) collective-permute-start(f32[32,16,1]{2,1,0:T(8,128)S(1)} %get-tuple-element.103), channel_id=1, source_target_pairs={{1,0},{3,2},{5,4},{7,6},{9,8},{11,10},{13,12},{15,14},{17,16},{19,... | collective-permute-start | bytes 6152 | tf_op jit(solution)/shard_map/ppermute | solution.py:27
  198.6 14.3 %collective-permute-start.23 = (f32[32,16,1]{2,1,0:T(8,128)S(1)}, f32[32,16,1]{2,1,0:T(8,128)S(1)}, u32[]{:S(2)}, u32[]{:S(2)}) collective-permute-start(f32[32,16,1]{2,1,0:T(8,128)S(1)} %get-tuple-element.104), channel_id=1, source_target_pairs={{0,1},{2,3},{4,5},{6,7},{8,9},{10,11},{12,13},{14,15},{16,17},{18,... | collective-permute-start | bytes 6152 | tf_op jit(solution)/shard_map/ppermute | solution.py:25
  199.9 13.8 %collective-permute-start.20 = (f32[32,1,128]{2,1,0:T(1,128)S(1)}, f32[32,1,128]{2,1,0:T(1,128)S(1)}, u32[]{:S(2)}, u32[]{:S(2)}) collective-permute-start(f32[32,1,128]{2,1,0:T(1,128)S(1)} %get-tuple-element.101), channel_id=1, source_target_pairs={{2,0},{4,2},{6,4},{8,6},{10,8},{12,10},{14,12},{16,14},{18,16},{20... | collective-permute-start | bytes 49160 | tf_op jit(solution)/shard_map/ppermute | solution.py:27
  201.2 12.5 %collective-permute-start.21 = (f32[32,1,128]{2,1,0:T(1,128)S(1)}, f32[32,1,128]{2,1,0:T(1,128)S(1)}, u32[]{:S(2)}, u32[]{:S(2)}) collective-permute-start(f32[32,1,128]{2,1,0:T(1,128)S(1)} %get-tuple-element.102), channel_id=1, source_target_pairs={{0,2},{2,4},{4,6},{6,8},{8,10},{10,12},{12,14},{14,16},{16,18},{18... | collective-permute-start | bytes 49160 | tf_op jit(solution)/shard_map/ppermute | solution.py:25
  206.7 6.2 %collective-permute-start.18 = (f32[1,16,128]{2,1,0:T(8,128)S(1)}, f32[1,16,128]{2,1,0:T(8,128)S(1)}, u32[]{:S(2)}, u32[]{:S(2)}) collective-permute-start(f32[1,16,128]{2,1,0:T(8,128)S(1)} %get-tuple-element.80), channel_id=1, source_target_pairs={{32,0},{64,32},{96,64},{128,96},{160,128},{192,160},{224,192},{33,... | collective-permute-start | bytes 24584 | tf_op jit(solution)/shard_map/ppermute | solution.py:27
  208.0 5.7 %collective-permute-start.19 = (f32[1,16,128]{2,1,0:T(8,128)S(1)}, f32[1,16,128]{2,1,0:T(8,128)S(1)}, u32[]{:S(2)}, u32[]{:S(2)}) collective-permute-start(f32[1,16,128]{2,1,0:T(8,128)S(1)} %get-tuple-element.81), channel_id=1, source_target_pairs={{0,32},{32,64},{64,96},{96,128},{128,160},{160,192},{192,224},{1,3... | collective-permute-start | bytes 24584 | tf_op jit(solution)/shard_map/ppermute | solution.py:25
  224.9 27.2 %all-to-all-start.1 = ((f32[16,16,256]{2,1,0:T(8,128)}), f32[16,16,256]{2,1,0:T(8,128)S(1)}, u32[]{:S(2)}, u32[]{:S(2)}) async-start(f32[16,16,256]{2,1,0:T(8,128)} %copy.47), calls=%async_computation.1 | async-start | bytes 524288 | tf_op jit(solution)/shard_map/all_to_all | solution.py:140
  261.6 24.2 %all-to-all-start.2 = ((f32[16,16,256]{2,1,0:T(8,128)}), f32[16,16,256]{2,1,0:T(8,128)S(1)}, u32[]{:S(2)}, u32[]{:S(2)}) async-start(f32[16,16,256]{2,1,0:T(8,128)} %copy.49), calls=%async_computation.2 | async-start | bytes 524288 | tf_op jit(solution)/shard_map/all_to_all | solution.py:152
  293.1 11.5 %all-to-all-start.3 = ((f32[16,16,256]{2,1,0:T(8,128)}), f32[16,16,256]{2,1,0:T(8,128)S(1)}, u32[]{:S(2)}, u32[]{:S(2)}) async-start(f32[16,16,256]{2,1,0:T(8,128)} %copy.61), calls=%async_computation.3 | async-start | bytes 524288 | tf_op jit(solution)/shard_map/all_to_all | solution.py:172
  (61 other events, 292.2 us)
where the time goes:
time: 356 us; the launch traced here: 351 us
  starting transfers between devices  114 us (32%)
  local copies, waits for them, and re-layouts  68 us (19%)
  other arithmetic  62.2 us (17%)
  matrix products  39.9 us (11%)
  waiting for transfers between devices  39.1 us (11%)
  blocking collectives  26.9 us (8%)
    ppermute x12, starting transfers between devices, padded_2(): lax.ppermute(tail, axis, [(i, (i + 1) % count) for i in range(ends)])  50.5 us
    add x8, other arithmetic, diffuse(): return center + time_step * middle * inflow  29.3 us
    dot_general x8, matrix products, one_block(): jnp.einsum('ck,nk->cn', lookup_table, one_hot, precision=lax.Precision.HI...  27.9 us
    ppermute x12, starting transfers between devices, padded_2(): lax.ppermute(head, axis, [((i + 1) % count, i) for i in range(ends)])  24.8 us
    all_to_all x2, starting transfers between devices, per_device(): lax.all_to_all(packed, ('gx', 'gz'), split_axis=0, concat_axis=0, tiled=T...  21.5 us
    all_to_all x1, starting transfers between devices, per_device(): lax.all_to_all(packed, 'gy', split_axis=0, concat_axis=0, tiled=True)  16.8 us
    mul x4, other arithmetic, diffuse(): return center + time_step * middle * inflow  15.1 us
    all_to_all x1, blocking collectives, per_device(): lax.all_to_all(packed, 'gy', split_axis=0, concat_axis=0, tiled=True)  14.1 us
  transfers between devices with their start and end apart: 27, of which 9 were waited for; matrix products, arithmetic and copies ran while one was open for 18% of the time, Pallas kernels for 0%

commit v1 on v0

v1 whole, which is shorter than its diff:
```python
import jax
import jax.numpy as jnp
import numpy as np
from jax import lax
from jax.experimental import pallas as pl
from jax.experimental.pallas import tpu as pltpu
from jax.sharding import PartitionSpec as P

N = 256
STEPS = 8
CLASSES = 4
HALO = STEPS + 1
XE = 16 + 2 * HALO
YE = 32
time_step = 0.08
norm_floor = 0.5
f32 = jnp.float32
bf16 = jnp.bfloat16
MESH = pl.DeviceIdType.MESH


def cosine_table():
    wave_number = np.arange(N, dtype=np.float32)[:, None]
    sample = np.arange(N, dtype=np.float32)[None, :]
    factor = np.where(wave_number == 0, np.sqrt(np.float32(1.0 / N)), np.sqrt(np.float32(2.0 / N)))
    angle = np.float32(np.pi) * wave_number * (np.float32(2.0) * sample + np.float32(1.0)) / np.float32(2.0 * N)
    return (factor * np.cos(angle)).astype(np.float32)


def eigen_values():
    wave_number = np.arange(N, dtype=np.float32)
    return (np.float32(2.0) - np.float32(2.0) * np.cos(np.float32(np.pi) * wave_number / np.float32(N))).astype(np.float32)


def halves(table):
    high = table.astype(jnp.bfloat16)
    low = (table - high.astype(np.float32)).astype(jnp.bfloat16)
    return np.stack([high, low])


def split(values):
    high = values.astype(bf16)
    return high, (values - high.astype(f32)).astype(bf16)


def product(left, right):
    dot = lambda a, b: jnp.dot(a, b, preferred_element_type=f32)
    return dot(left[0], right[0]) + (dot(left[1], right[0]) + dot(left[0], right[1]))


def swap8(tile):
    row = lax.broadcasted_iota(jnp.int32, (8, 128), 0)
    group = lax.broadcasted_iota(jnp.int32, (8, 128), 1) // 16
    for bit in (1, 2, 4):
        row_bit = (row // bit) % 2
        group_bit = (group // bit) % 2
        if bit == 4:
            other = pltpu.roll(pltpu.roll(tile, 4, 0), 64, 1)
        else:
            forth = pltpu.roll(pltpu.roll(tile, bit, 0), 128 - 16 * bit, 1)
            back = pltpu.roll(pltpu.roll(tile, 8 - bit, 0), 16 * bit, 1)
            other = jnp.where(row_bit == 1, forth, back)
        tile = jnp.where(row_bit == group_bit, tile, other)
    return tile


def halo_copies(field, rows, ext, row_ext, send_sem, recv_sem):
    gx, gy, gz = lax.axis_index("gx"), lax.axis_index("gy"), lax.axis_index("gz")
    lanes = pl.ds(pl.multiple_of(gz * 128, 128), 128)
    copies = []
    for dy in (1, -1, 0):
        src_rows = {1: pl.ds(8, 8), -1: pl.ds(0, 8), 0: pl.ds(0, 16)}[dy]
        dst_rows = {1: pl.ds(0, 8), -1: pl.ds(24, 8), 0: pl.ds(8, 16)}[dy]
        to_y = lax.rem(gy + dy + 16, 16)
        for other in (0, 1):
            core = 1 - gz if other else gz
            to_x = lax.rem(gx + 1 - 2 * core + 8, 8)
            parts = [
                (field.at[:, pl.ds(7 * core, 25), src_rows, :], ext.at[:, pl.ds(9 * (1 - core), 25), dst_rows, lanes], gx),
                (field.at[:, pl.ds(23 * (1 - core), 9), src_rows, :], ext.at[:, pl.ds(25 * core, 9), dst_rows, lanes], to_x),
            ]
            if dy:
                side = 0 if dy == 1 else 1
                parts += [
                    (rows.at[side], row_ext.at[side, :, pl.ds(16, 32), lanes], gx),
                    (rows.at[side, :, pl.ds(pl.multiple_of(16 * (1 - core), 16), 16), :],
                     row_ext.at[side, :, pl.ds(pl.multiple_of(48 * core, 16), 16), lanes], to_x),
                ]
            for index, (src, dst, x) in enumerate(parts):
                slot = len(copies)
                if dy == 0 and other == 0 and index == 0:
                    copies.append(pltpu.make_async_copy(src, dst, recv_sem.at[slot]))
                else:
                    copies.append(pltpu.make_async_remote_copy(
                        src, dst, send_sem.at[slot], recv_sem.at[slot],
                        device_id=(x, to_y, core), device_id_type=MESH))
    return copies


def greet_halo(barrier):
    gx, gy, gz = lax.axis_index("gx"), lax.axis_index("gy"), lax.axis_index("gz")
    from_x = lax.rem(gx + 2 * gz - 1 + 8, 8)
    count = 0
    for dy in (1, -1, 0):
        y = lax.rem(gy + dy + 16, 16)
        for core in (0, 1):
            pl.semaphore_signal(barrier, inc=1, device_id=(from_x, y, core), device_id_type=MESH)
            count += 1
        pl.semaphore_signal(barrier, inc=1, device_id=(gx, y, 1 - gz), device_id_type=MESH)
        count += 1
        if dy:
            pl.semaphore_signal(barrier, inc=1, device_id=(gx, y, gz), device_id_type=MESH)
            count += 1
    return count


def fill_field(ids_ref, class_ref, cond_ref, table_ref, field, rows):
    def plane(i, _):
        classes = class_ref[i]
        value = jnp.full(classes.shape, table_ref[0], f32)
        for k in range(1, CLASSES):
            value = jnp.where(classes == k, table_ref[k], value)
        field[0, i] = jnp.sqrt(value * cond_ref[i])
        field[1, i] = ids_ref[i].astype(f32)
        return 0
    lax.fori_loop(0, 32, plane, 0)
    for which in range(2):
        rows[0, which] = field[which, :, 7, :]
        rows[1, which] = field[which, :, 8, :]


def lookup(ids_float, tables):
    index = ids_float.astype(jnp.int32) - 1
    low = jnp.bitwise_and(index, 127)
    found = []
    for first, second in tables:
        a = jnp.take_along_axis(first, low, axis=1)
        b = jnp.take_along_axis(second, low, axis=1)
        found.append(jnp.where(index < 0, 0.0, jnp.where(index < 128, a, b)))
    return found


def z_sides(values):
    lane = lax.broadcasted_iota(jnp.int32, (values.shape[0], 128), 1)
    low, high = values[:, :128], values[:, 128:]
    low_up, high_up = pltpu.roll(low, 1, 1), pltpu.roll(high, 1, 1)
    low_down, high_down = pltpu.roll(low, 127, 1), pltpu.roll(high, 127, 1)
    before = (jnp.where(lane == 0, 0.0, low_up), jnp.where(lane == 0, low_up, high_up))
    after = (jnp.where(lane == 127, high_down, low_down), jnp.where(lane == 127, 0.0, high_down))
    return before, after


def heat_part(normals_ref, ext, row_ext, forward_ref, out_ref, root, gain, keep, wa, wb, row_root, row_w, div, mixed):
    gx, gy, gz = lax.axis_index("gx"), lax.axis_index("gy"), lax.axis_index("gz")
    x0 = gx * 32 + gz * 16
    y0 = gy * 16

    def tables(r):
        return [tuple(jnp.broadcast_to(normals_ref[j:j + 1, h * 128:(h + 1) * 128], (r, 128)) for h in range(2)) for j in range(3)]

    y_of = lax.broadcasted_iota(jnp.int32, (YE, 256), 0) + (y0 - 8)
    y_inside = jnp.logical_and(y_of >= 0, y_of < N)

    def start(i, _):
        x = x0 - HALO + i
        inside = jnp.logical_and(y_inside, jnp.logical_and(x >= 0, x < N))
        value = jnp.where(inside, ext[0, i], 0.0)
        root[i] = value
        for h in range(2):
            lanes = pl.ds(h * 128, 128)
            found = lookup(ext[1, i, :, lanes], tables(YE))
            for j in range(3):
                wa[j, i, :, lanes] = found[j] * value[:, h * 128:(h + 1) * 128]
        return 0
    lax.fori_loop(0, XE, start, 0)

    x_of = lax.broadcasted_iota(jnp.int32, (64, 256), 0) + (gx * 32 - 16)
    x_inside = jnp.logical_and(x_of >= 0, x_of < N)
    for side in range(2):
        y = y0 - 9 if side == 0 else y0 + 24
        inside = jnp.logical_and(x_inside, jnp.logical_and(y >= 0, y < N))
        value = jnp.where(inside, row_ext[side, 0], 0.0)
        row_root[side] = value
        for h in range(2):
            lanes = pl.ds(h * 128, 128)
            found = lookup(row_ext[side, 1, :, lanes], tables(64))
            for j in range(3):
                row_w[side, j, :, lanes] = found[j] * value[:, h * 128:(h + 1) * 128]

    y_index = lax.broadcasted_iota(jnp.int32, (YE, 256), 0)

    def around(values, before_row=None, after_row=None):
        up, down = pltpu.roll(values, 1, 0), pltpu.roll(values, YE - 1, 0)
        if before_row is not None:
            up = jnp.where(y_index == 0, before_row, up)
            down = jnp.where(y_index == YE - 1, after_row, down)
        before, after = z_sides(values)
        side = jnp.concatenate([before[0] + after[0], before[1] + after[1]], axis=1)
        return (up + down) + side

    def coefficients(i, _):
        r = i + 7 + 16 * gz
        center = root[i]
        total = around(center, row_root[0, pl.ds(r, 1), :], row_root[1, pl.ds(r, 1), :]) + (root[i - 1] + root[i + 1])
        keep[i] = 1.0 - time_step * center * total
        gain[i] = time_step * center * center
        return 0
    lax.fori_loop(1, XE - 1, coefficients, 0)

    for step in range(1, STEPS + 1):
        src, dst = (wa, wb) if step % 2 else (wb, wa)

        def plane(i, _, src=src, dst=dst, step=step):
            a, d = keep[i], gain[i]
            r = i + 7 + 16 * gz
            for j in range(3):
                center = src[j, i]
                if step == 1:
                    total = around(center, row_w[0, j, pl.ds(r, 1), :], row_w[1, j, pl.ds(r, 1), :])
                else:
                    total = around(center)
                total = total + (src[j, i - 1] + src[j, i + 1])
                dst[j, i] = a * center + d * total
            return 0
        lax.fori_loop(step, XE - step, plane, 0)

    def unit(i, _):
        w = [wa[j, i] for j in range(3)]
        size = jnp.sqrt(w[0] * w[0] + w[1] * w[1] + w[2] * w[2])
        floor = jnp.maximum(jnp.maximum(size, norm_floor * root[i]), 1e-30)
        scale = 0.5 / floor
        for j in range(3):
            wb[j, i] = w[j] * scale
        return 0
    lax.fori_loop(STEPS, XE - STEPS, unit, 0)

    def divergence(k, _):
        i = k + HALO
        u1 = wb[1, i]
        before, after = z_sides(wb[2, i])
        part_z = jnp.concatenate([after[0] - before[0], after[1] - before[1]], axis=1)
        value = (wb[0, i + 1] - wb[0, i - 1]) + (pltpu.roll(u1, YE - 1, 0) - pltpu.roll(u1, 1, 0)) + part_z
        for h in range(2):
            div[h, pl.ds(pl.multiple_of(k * 16, 16), 16), :] = value[8:24, h * 128:(h + 1) * 128]
        return 0
    lax.fori_loop(0, 16, divergence, 0)

    lines = jnp.concatenate(
        [jnp.concatenate([div[h, pl.ds(y, 16, stride=16), :] for y in range(16)], axis=0) for h in range(2)], axis=1)
    mixed[...] = product(split(lines), (forward_ref[0], forward_ref[1]))

    def spread(y, _):
        for xh in range(2):
            for ah in range(2):
                tile = mixed[pl.ds(pl.multiple_of(y * 16 + xh * 8, 8), 8), pl.ds(ah * 128, 128)]
                out_ref[xh, pl.ds(ah * 128 + y, 8, stride=16), :] = swap8(tile)
        return 0
    lax.fori_loop(0, 16, spread, 0)


def y_group(index):
    return (lax.axis_index("gx"), index, lax.axis_index("gz"))


def x_group(index):
    return (index // 2, lax.axis_index("gy"), index % 2)


def exchange(src, dst, me, where, send_sem, recv_sem):
    def copy(d):
        to = lax.rem(me + d, 16)
        return pltpu.make_async_remote_copy(
            src.at[:, pl.ds(pl.multiple_of(to * 16, 16), 16), :],
            dst.at[:, pl.ds(pl.multiple_of(me * 16, 16), 16), :],
            send_sem.at[d], recv_sem.at[d], device_id=where(to), device_id_type=MESH)

    def start(d, _):
        copy(d).start()
        return 0
    lax.fori_loop(1, 16, start, 0)
    own = pl.ds(pl.multiple_of(me * 16, 16), 16)
    dst[:, own, :] = src[:, own, :]

    def wait(d, _):
        copy(d).wait()
        return 0
    lax.fori_loop(1, 16, wait, 0)


def whole(ref):
    return jnp.concatenate([ref[0], ref[1]], axis=1)


def turn(values, mixed, dst):
    mixed[...] = values

    def block(b, _):
        for rh in range(2):
            for gh in range(2):
                tile = mixed[pl.ds(pl.multiple_of(b * 16 + rh * 8, 8), 8), pl.ds(gh * 128, 128)]
                dst[rh, pl.ds(pl.multiple_of(b * 16 + gh * 8, 8), 8), :] = swap8(tile)
        return 0
    lax.fori_loop(0, 16, block, 0)


def greet_groups(barrier):
    gx, gy, gz = lax.axis_index("gx"), lax.axis_index("gy"), lax.axis_index("gz")
    group = gx * 2 + gz

    def greet(d, _):
        pl.semaphore_signal(barrier, inc=1, device_id=y_group(lax.rem(gy + d, 16)), device_id_type=MESH)
        pl.semaphore_signal(barrier, inc=1, device_id=x_group(lax.rem(group + d, 16)), device_id_type=MESH)
        return 0
    lax.fori_loop(1, 16, greet, 0)
    return 30


def solve_part(s1, forward_ref, cosine_ref, eigen_x, eigen_y, eigen_z, out_ref, r2, s2, r3, s3, r4, s4, r5, lines, own_out, peer_out, mixed,
               send_sem, recv_sem, last_send, last_recv):
    gx, gy, gz = lax.axis_index("gx"), lax.axis_index("gy"), lax.axis_index("gz")
    group = gx * 2 + gz
    cosine = (cosine_ref[0], cosine_ref[1])
    forward = (forward_ref[0], forward_ref[1])
    exchange(s1, r2, gy, y_group, send_sem.at[0], recv_sem.at[0])
    turn(product(cosine, split(whole(r2))), mixed, s2)
    exchange(s2, r3, group, x_group, send_sem.at[1], recv_sem.at[1])
    spectrum = product(cosine, split(whole(r3)))
    rest = eigen_y[pl.ds(group, 1), :] + eigen_z[pl.ds(gy, 1), :]
    eigen = jnp.concatenate([eigen_x[...], eigen_x[...]], axis=1)
    solved = -spectrum / (eigen + rest + 4.0 / (N * N))
    turn(product(forward, split(solved)), mixed, s3)
    exchange(s3, r4, group, x_group, send_sem.at[2], recv_sem.at[2])
    values = product(forward, split(whole(r4)))
    for h in range(2):
        s4[h] = values[:, h * 128:(h + 1) * 128]
    exchange(s4, r5, gy, y_group, send_sem.at[3], recv_sem.at[3])

    def gather(y, _):
        for xh in range(2):
            for ah in range(2):
                tile = r5[xh, pl.ds(ah * 128 + y, 8, stride=16), :]
                lines[pl.ds(pl.multiple_of(y * 16 + xh * 8, 8), 8), pl.ds(ah * 128, 128)] = swap8(tile)
        return 0
    lax.fori_loop(0, 16, gather, 0)
    values = product(split(lines[...]), cosine)
    first = gz == 0
    mine = jnp.where(first, values[:, :128], values[:, 128:])
    theirs = jnp.where(first, values[:, 128:], values[:, :128])
    for y in range(16):
        peer_out[pl.ds(y, 16, stride=16), :] = theirs[y * 16:(y + 1) * 16]
    rows = pl.ds(pl.multiple_of(gz * 256, 256), 256)
    copy = pltpu.make_async_remote_copy(
        peer_out, out_ref.at[rows, :], last_send, last_recv, device_id=(gx, gy, 1 - gz), device_id_type=MESH)
    copy.start()
    for y in range(16):
        own_out[pl.ds(y, 16, stride=16), :] = mine[y * 16:(y + 1) * 16]
    out_ref[rows, :] = own_out[...]
    copy.wait()


VM = pl.BlockSpec(memory_space=pltpu.VMEM)
SM = pl.BlockSpec(memory_space=pltpu.SMEM)
DMA = pltpu.SemaphoreType.DMA
LIMIT = 48 * 1024 * 1024


def vmem(*shape):
    return pltpu.VMEM(shape, f32)


def first_kernel(ids_ref, class_ref, cond_ref, table_ref, ext, row_ext, field, rows, send_sem, recv_sem):
    barrier = pltpu.get_barrier_semaphore()
    count = greet_halo(barrier)
    fill_field(ids_ref, class_ref, cond_ref, table_ref, field, rows)
    pl.semaphore_wait(barrier, count)
    copies = halo_copies(field, rows, ext, row_ext, send_sem, recv_sem)
    for copy in copies:
        copy.start()
    for copy in copies:
        copy.wait()


def third_kernel(s1, *rest):
    barrier = pltpu.get_barrier_semaphore()
    count = greet_groups(barrier)
    pl.semaphore_wait(barrier, count)
    solve_part(s1, *rest)


def per_device(surface_ids, class_map, conductivity, normals, class_table):
    cosine = cosine_table()
    eigen = eigen_values()
    cosine_pair, forward_pair = jnp.asarray(halves(cosine)), jnp.asarray(halves(cosine.T.copy()))
    eigen_x = jnp.asarray(np.repeat(eigen[:, None], 128, axis=1))
    eigen_y = jnp.asarray(np.repeat(eigen.reshape(16, 16), 16, axis=1))
    eigen_z = jnp.asarray(np.tile(eigen.reshape(16, 16), (1, 16)))
    ext, row_ext = pl.pallas_call(
        first_kernel,
        out_shape=(jax.ShapeDtypeStruct((2, XE, YE, 256), f32), jax.ShapeDtypeStruct((2, 2, 64, 256), f32)),
        in_specs=[VM, VM, VM, SM], out_specs=(VM, VM),
        scratch_shapes=[vmem(2, 32, 16, 128), vmem(2, 2, 32, 128), DMA((20,)), DMA((20,))],
        compiler_params=pltpu.CompilerParams(collective_id=0, has_side_effects=True, vmem_limit_bytes=LIMIT),
    )(surface_ids, class_map, conductivity, class_table)
    s1 = pl.pallas_call(
        heat_part,
        out_shape=jax.ShapeDtypeStruct((2, 256, 128), f32),
        in_specs=[VM, VM, VM, VM], out_specs=VM,
        scratch_shapes=[vmem(XE, YE, 256), vmem(XE, YE, 256), vmem(XE, YE, 256), vmem(3, XE, YE, 256), vmem(3, XE, YE, 256),
                        vmem(2, 64, 256), vmem(2, 3, 64, 256), vmem(2, 256, 128), vmem(256, 256)],
        compiler_params=pltpu.CompilerParams(vmem_limit_bytes=LIMIT),
    )(normals, ext, row_ext, forward_pair)
    out = pl.pallas_call(
        third_kernel,
        out_shape=jax.ShapeDtypeStruct((512, 128), f32),
        in_specs=[VM] * 6, out_specs=VM,
        scratch_shapes=[vmem(2, 256, 128) for _ in range(7)] + [vmem(256, 256), vmem(256, 128), vmem(256, 128), vmem(256, 256),
                        DMA((4, 16)), DMA((4, 16)), DMA(()), DMA(())],
        compiler_params=pltpu.CompilerParams(collective_id=1, has_side_effects=True, vmem_limit_bytes=LIMIT),
    )(s1, forward_pair, cosine_pair, eigen_x, eigen_y, eigen_z)
    return out.reshape(32, 16, 128)


def solution(mesh):
    spec = P("gx", "gy", "gz")
    return jax.shard_map(
        per_device, mesh=mesh, in_specs=(spec, spec, spec, P(), P()), out_specs=spec, check_vma=False
    )
```

time: 356 us -> 127 us (0.36); the launches traced: 351 us -> 127 us
  Pallas kernels: 0 us -> 121 us
  starting transfers between devices: 114 us -> 0 us
  other arithmetic: 62.2 us -> 0 us
  local copies, waits for them, and re-layouts: 68 us -> 5.9 us
  matrix products: 39.9 us -> 0 us
  waiting for transfers between devices: 39.1 us -> 0 us
  blocking collectives: 26.9 us -> 0 us
    pallas_call x0 -> x3, Pallas kernels: none -> 121 us  [the longest x1 47.2 us: per_device(): pl.pallas_call(third_kernel, out_shape=jax.ShapeDtypeStruct((512, 128), f...]
    ppermute x24 -> x0, starting transfers between devices: 75.3 us -> none  [the longest x12 50.5 us: padded_2(): lax.ppermute(tail, axis, [(i, (i + 1) % count) for i in range(ends)])]
    dot_general x14 -> x0, matrix products: 39.9 us -> none  [the longest x8 27.9 us: one_block(): jnp.einsum('ck,nk->cn', lookup_table, one_hot, precision=lax.Precision.HI...]
    all_to_all x3 -> x0, starting transfers between devices: 38.3 us -> none  [the longest x2 21.5 us: per_device(): lax.all_to_all(packed, ('gx', 'gz'), split_axis=0, concat_axis=0, tiled=T...]
    add x13 -> x0, other arithmetic: 29.8 us -> none  [the longest x8 29.3 us: diffuse(): return center + time_step * middle * inflow]
    all_to_all x3 -> x0, blocking collectives: 26.9 us -> none  [the longest x1 14.1 us: per_device(): lax.all_to_all(packed, 'gy', split_axis=0, concat_axis=0, tiled=True)]
    all_to_all x3 -> x0, waiting for transfers between devices: 24.1 us -> none  [the longest x2 14 us: per_device(): lax.all_to_all(packed, ('gx', 'gz'), split_axis=0, concat_axis=0, tiled=T...]
    slice x17 -> x0, local copies, waits for them, and re-layouts: 18.6 us -> none  [the longest x8 9.61 us: padded_2(): lax.slice_in_dim(cells, cells.shape[dim] - width, cells.shape[dim], axis=...]
  transfers between devices with their start and end apart: 27 -> 0, of which waited for: 9 -> 0; matrix products, arithmetic and copies ran while one was open for 18% -> 0% of each run, Pallas kernels for 0% -> 0%
where the time goes in v1:
time: 127 us
  Pallas kernels  121 us (95%)
  local copies, waits for them, and re-layouts  5.9 us (5%)
    pallas_call x1, Pallas kernels, per_device(): pl.pallas_call(third_kernel, out_shape=jax.ShapeDtypeStruct((512, 128), f...  47.2 us
    pallas_call x1, Pallas kernels, per_device(): pl.pallas_call(heat_part, out_shape=jax.ShapeDtypeStruct((2, 256, 128), f...  41.3 us
    pallas_call x1, Pallas kernels, per_device(): pl.pallas_call(first_kernel, out_shape=(jax.ShapeDtypeStruct((2, XE, YE,...  32 us
    unnamed x21, local copies, waits for them, and re-layouts  5.9 us

profile of v1, /device:TPU:1, one launch (start us, length us, event | category | flops | bytes accessed | tf_op | source)
XLA Modules:
  0.0 126.5 jit_solution(643008267385671224)
XLA Ops:
  0.0 0.0 copy-start.1
  0.0 0.0 copy-start.2
  0.0 1.0 copy-done.2
  1.0 0.0 copy-start.3
  1.0 0.9 copy-done.3
  1.9 0.0 copy-start.4
  1.9 0.9 copy-done.4
  2.9 0.0 copy-start.9
  2.9 0.7 copy-done.9
  3.6 0.0 copy-start.5
  3.6 0.0 copy-start.6
  3.6 0.0 copy-start.7
  3.6 32.0 %shard_map.100 = (f32[2,34,32,256]{3,2,1,0:T(8,128)S(1)}, f32[2,2,64,256]{3,2,1,0:T(8,128)S(1)}) custom-call(s32[32,16,128]{2,1,0:T(8,128)S(1)} %copy-done.2, s32[32,16,128]{2,1,0:T(8,128)S(1)} %copy-done.3, f32[32,16,128]{2,1,0:T(8,128)S(1)} %copy-done.4, f32[4]{0:T(128)S(1)} %copy-done.9), custom_call_target="tpu_custom_call" | custom-call | tf_op jit(solution)/shard_map/pallas_call | solution.py:397
  35.6 0.0 copy-start
  35.6 0.9 copy-done
  36.6 0.0 copy-start.8
  36.6 0.7 copy-done.8
  37.3 41.3 %shard_map.101.s1 = f32[2,256,128]{2,1,0:T(8,128)S(1)} custom-call(f32[3,256]{1,0:T(4,128)S(1)} %copy-done.8, f32[2,34,32,256]{3,2,1,0:T(8,128)S(1)} %get-tuple-element.7.ext, f32[2,2,64,256]{3,2,1,0:T(8,128)S(1)} %get-tuple-element.8.row_ext, bf16[2,256,256]{2,1,0:T(8,128)(2,1)S(1)} %copy-done), custom_call_target="tpu_custom_call" | custom-call | tf_op jit(solution)/shard_map/pallas_call | solution.py:404
  78.5 0.0 copy-done.1
  78.5 0.0 copy-done.5
  78.6 0.0 copy-done.6
  78.6 0.0 copy-done.7
  78.6 47.2 %shard_map.102 = f32[512,128]{1,0:T(8,128)S(1)} custom-call(f32[2,256,128]{2,1,0:T(8,128)S(1)} %shard_map.101.s1, bf16[2,256,256]{2,1,0:T(8,128)(2,1)S(1)} %copy-done, bf16[2,256,256]{2,1,0:T(8,128)(2,1)S(1)} %copy-done.1, f32[256,128]{1,0:T(8,128)S(1)} %copy-done.5, f32[16,256]{1,0:T(8,128)S(1)} %copy-done.7, f32[16,256]{1,0:T(8,128)S(1)} %copy-done.6), custom_call_target="tpu_custom_call" | custom-call | tf_op jit(solution)/shard_map/pallas_call | solution.py:412
  125.8 0.7 copy.12
Async XLA Ops:
  0.0 78.5 %copy-start.1 = (bf16[2,256,256]{2,1,0:T(8,128)(2,1)S(1)}, bf16[2,256,256]{2,1,0:T(8,128)(2,1)}, u32[]{:S(2)}) copy-start(bf16[2,256,256]{2,1,0:T(8,128)(2,1)} %constant.10.clone.rest_1_) | copy-start | bytes 786436
  0.0 1.0 copy-start.2
  1.0 0.9 copy-start.3
  1.9 0.9 copy-start.4
  2.9 0.7 copy-start.9
  3.6 75.0 %copy-start.5 = (f32[256,128]{1,0:T(8,128)S(1)}, f32[256,128]{1,0:T(8,128)}, u32[]{:S(2)}) copy-start(f32[256,128]{1,0:T(8,128)} %constant.12.clone.rest_2_) | copy-start | bytes 393220
  3.6 75.0 %copy-start.6 = (f32[16,256]{1,0:T(8,128)S(1)}, f32[16,256]{1,0:T(8,128)}, u32[]{:S(2)}) copy-start(f32[16,256]{1,0:T(8,128)} %constant.14.clone.rest_4_) | copy-start | bytes 49156
  3.6 75.0 %copy-start.7 = (f32[16,256]{1,0:T(8,128)S(1)}, f32[16,256]{1,0:T(8,128)}, u32[]{:S(2)}) copy-start(f32[16,256]{1,0:T(8,128)} %constant.13.clone.rest_3_) | copy-start | bytes 49156
  35.6 1.0 copy-start
  36.6 0.7 copy-start.8

commit v2 on v1

--- a/solution.py
+++ b/solution.py
@@ -140,17 +140,48 @@
     return found
 
 
-def z_sides(values):
-    lane = lax.broadcasted_iota(jnp.int32, (values.shape[0], 128), 1)
-    low, high = values[:, :128], values[:, 128:]
+SWAP_UNROLL = 16
+UNROLL = 6
+UNALIGNED = True
+LOOKUP_UNROLL = 4
+
+
+def z_sum(low, high):
+    lane = lax.broadcasted_iota(jnp.int32, low.shape, 1)
     low_up, high_up = pltpu.roll(low, 1, 1), pltpu.roll(high, 1, 1)
     low_down, high_down = pltpu.roll(low, 127, 1), pltpu.roll(high, 127, 1)
-    before = (jnp.where(lane == 0, 0.0, low_up), jnp.where(lane == 0, low_up, high_up))
-    after = (jnp.where(lane == 127, high_down, low_down), jnp.where(lane == 127, 0.0, high_down))
-    return before, after
-
-
-def heat_part(normals_ref, ext, row_ext, forward_ref, out_ref, root, gain, keep, wa, wb, row_root, row_w, div, mixed):
+    first, last = lane == 0, lane == 127
+    return (jnp.where(first, 0.0, low_up) + jnp.where(last, high_down, low_down),
+            jnp.where(first, low_up, high_up) + jnp.where(last, 0.0, high_down))
+
+
+def z_difference(low, high):
+    lane = lax.broadcasted_iota(jnp.int32, low.shape, 1)
+    low_up, high_up = pltpu.roll(low, 1, 1), pltpu.roll(high, 1, 1)
+    low_down, high_down = pltpu.roll(low, 127, 1), pltpu.roll(high, 127, 1)
+    first, last = lane == 0, lane == 127
+    return (jnp.where(last, high_down, low_down) - jnp.where(first, 0.0, low_up),
+            jnp.where(last, 0.0, high_down) - jnp.where(first, low_up, high_up))
+
+
+BODY = pl.ds(8, YE)
+
+
+def neighbours(ref, lead, i):
+    center = [ref[lead + (h, i, BODY)] for h in range(2)]
+    sides = z_sum(*center)
+    total = []
+    for h in range(2):
+        if UNALIGNED:
+            y = ref[lead + (h, i, pl.ds(7, YE))] + ref[lead + (h, i, pl.ds(9, YE))]
+        else:
+            y = pltpu.roll(center[h], 1, 0) + pltpu.roll(center[h], YE - 1, 0)
+        x = ref[lead + (h, i - 1, BODY)] + ref[lead + (h, i + 1, BODY)]
+        total.append((x + y) + sides[h])
+    return center, total
+
+
+def heat_part(normals_ref, ext, row_ext, forward_ref, out_ref, root, gain, keep, wa, wb, div, mixed):
     gx, gy, gz = lax.axis_index("gx"), lax.axis_index("gy"), lax.axis_index("gz")
     x0 = gx * 32 + gz * 16
     y0 = gy * 16
@@ -158,92 +189,85 @@
     def tables(r):
         return [tuple(jnp.broadcast_to(normals_ref[j:j + 1, h * 128:(h + 1) * 128], (r, 128)) for h in range(2)) for j in range(3)]
 
-    y_of = lax.broadcasted_iota(jnp.int32, (YE, 256), 0) + (y0 - 8)
+    y_of = lax.broadcasted_iota(jnp.int32, (YE, 128), 0) + (y0 - 8)
     y_inside = jnp.logical_and(y_of >= 0, y_of < N)
 
     def start(i, _):
         x = x0 - HALO + i
-        inside = jnp.logical_and(y_inside, jnp.logical_and(x >= 0, x < N))
-        value = jnp.where(inside, ext[0, i], 0.0)
-        root[i] = value
+        x_in = jnp.logical_and(x >= 0, x < N)
+        inside = jnp.logical_and(y_inside, x_in)
+        r = i + 7 + 16 * gz
+        done = []
         for h in range(2):
             lanes = pl.ds(h * 128, 128)
+            value = jnp.where(inside, ext[0, i, :, lanes], 0.0)
             found = lookup(ext[1, i, :, lanes], tables(YE))
+            done.append((value, [found[j] * value for j in range(3)]))
+        for h in range(2):
+            root[h, i, BODY] = done[h][0]
             for j in range(3):
-                wa[j, i, :, lanes] = found[j] * value[:, h * 128:(h + 1) * 128]
-        return 0
-    lax.fori_loop(0, XE, start, 0)
-
-    x_of = lax.broadcasted_iota(jnp.int32, (64, 256), 0) + (gx * 32 - 16)
+                wa[j, h, i, BODY] = done[h][1][j]
+        return 0
+    lax.fori_loop(0, XE, start, 0, unroll=LOOKUP_UNROLL)
+
+    x_of = lax.broadcasted_iota(jnp.int32, (40, 128), 0) + (x0 - HALO)
     x_inside = jnp.logical_and(x_of >= 0, x_of < N)
+    wide = pl.ds(pl.multiple_of(16 * gz, 8), 48)
     for side in range(2):
         y = y0 - 9 if side == 0 else y0 + 24
         inside = jnp.logical_and(x_inside, jnp.logical_and(y >= 0, y < N))
-        value = jnp.where(inside, row_ext[side, 0], 0.0)
-        row_root[side] = value
+        row = 7 if side == 0 else 40
         for h in range(2):
             lanes = pl.ds(h * 128, 128)
-            found = lookup(row_ext[side, 1, :, lanes], tables(64))
+            value = jnp.where(inside, row_ext[side, 0, wide, lanes][7:47], 0.0)
+            found = lookup(row_ext[side, 1, wide, lanes][7:47], tables(40))
+            root[h, :, row, :] = value[:XE]
             for j in range(3):
-                row_w[side, j, :, lanes] = found[j] * value[:, h * 128:(h + 1) * 128]
-
-    y_index = lax.broadcasted_iota(jnp.int32, (YE, 256), 0)
-
-    def around(values, before_row=None, after_row=None):
-        up, down = pltpu.roll(values, 1, 0), pltpu.roll(values, YE - 1, 0)
-        if before_row is not None:
-            up = jnp.where(y_index == 0, before_row, up)
-            down = jnp.where(y_index == YE - 1, after_row, down)
-        before, after = z_sides(values)
-        side = jnp.concatenate([before[0] + after[0], before[1] + after[1]], axis=1)
-        return (up + down) + side
+                wa[j, h, :, row, :] = (found[j] * value)[:XE]
+                wb[j, h, :, row, :] = jnp.zeros((XE, 128), f32)
 
     def coefficients(i, _):
-        r = i + 7 + 16 * gz
-        center = root[i]
-        total = around(center, row_root[0, pl.ds(r, 1), :], row_root[1, pl.ds(r, 1), :]) + (root[i - 1] + root[i + 1])
-        keep[i] = 1.0 - time_step * center * total
-        gain[i] = time_step * center * center
-        return 0
-    lax.fori_loop(1, XE - 1, coefficients, 0)
+        center, total = neighbours(root, (), i)
+        for h in range(2):
+            keep[h, i] = 1.0 - time_step * center[h] * total[h]
+            gain[h, i] = time_step * center[h] * center[h]
+        return 0
+    lax.fori_loop(1, XE - 1, coefficients, 0, unroll=UNROLL)
 
     for step in range(1, STEPS + 1):
         src, dst = (wa, wb) if step % 2 else (wb, wa)
 
-        def plane(i, _, src=src, dst=dst, step=step):
-            a, d = keep[i], gain[i]
-            r = i + 7 + 16 * gz
+        def plane(i, _, src=src, dst=dst):
+            done = []
             for j in range(3):
-                center = src[j, i]
-                if step == 1:
-                    total = around(center, row_w[0, j, pl.ds(r, 1), :], row_w[1, j, pl.ds(r, 1), :])
-                else:
-                    total = around(center)
-                total = total + (src[j, i - 1] + src[j, i + 1])
-                dst[j, i] = a * center + d * total
+                center, total = neighbours(src, (j,), i)
+                for h in range(2):
+                    done.append((j, h, keep[h, i] * center[h] + gain[h, i] * total[h]))
+            for j, h, value in done:
+                dst[j, h, i, BODY] = value
             return 0
-        lax.fori_loop(step, XE - step, plane, 0)
+        lax.fori_loop(step, XE - step, plane, 0, unroll=UNROLL)
 
     def unit(i, _):
-        w = [wa[j, i] for j in range(3)]
-        size = jnp.sqrt(w[0] * w[0] + w[1] * w[1] + w[2] * w[2])
-        floor = jnp.maximum(jnp.maximum(size, norm_floor * root[i]), 1e-30)
-        scale = 0.5 / floor
-        for j in range(3):
-            wb[j, i] = w[j] * scale
-        return 0
-    lax.fori_loop(STEPS, XE - STEPS, unit, 0)
+        for h in range(2):
+            w = [wa[j, h, i, BODY] for j in range(3)]
+            size = jnp.sqrt(w[0] * w[0] + w[1] * w[1] + w[2] * w[2])
+            floor = jnp.maximum(jnp.maximum(size, norm_floor * root[h, i, BODY]), 1e-30)
+            scale = 0.5 / floor
+            for j in range(3):
+                wb[j, h, i, BODY] = w[j] * scale
+        return 0
+    lax.fori_loop(STEPS, XE - STEPS, unit, 0, unroll=UNROLL)
 
     def divergence(k, _):
         i = k + HALO
-        u1 = wb[1, i]
-        before, after = z_sides(wb[2, i])
-        part_z = jnp.concatenate([after[0] - before[0], after[1] - before[1]], axis=1)
-        value = (wb[0, i + 1] - wb[0, i - 1]) + (pltpu.roll(u1, YE - 1, 0) - pltpu.roll(u1, 1, 0)) + part_z
-        for h in range(2):
-            div[h, pl.ds(pl.multiple_of(k * 16, 16), 16), :] = value[8:24, h * 128:(h + 1) * 128]
-        return 0
-    lax.fori_loop(0, 16, divergence, 0)
+        part_z = z_difference(*[wb[2, h, i, pl.ds(16, 16)] for h in range(2)])
+        for h in range(2):
+            part_x = wb[0, h, i + 1, pl.ds(16, 16)] - wb[0, h, i - 1, pl.ds(16, 16)]
+            part_y = wb[1, h, i, pl.ds(17, 16)] - wb[1, h, i, pl.ds(15, 16)]
+            div[h, pl.ds(pl.multiple_of(k * 16, 16), 16), :] = part_x + part_y + part_z[h]
+        return 0
+    lax.fori_loop(0, 16, divergence, 0, unroll=UNROLL)
 
     lines = jnp.concatenate(
         [jnp.concatenate([div[h, pl.ds(y, 16, stride=16), :] for y in range(16)], axis=0) for h in range(2)], axis=1)
@@ -255,7 +279,7 @@
                 tile = mixed[pl.ds(pl.multiple_of(y * 16 + xh * 8, 8), 8), pl.ds(ah * 128, 128)]
                 out_ref[xh, pl.ds(ah * 128 + y, 8, stride=16), :] = swap8(tile)
         return 0
-    lax.fori_loop(0, 16, spread, 0)
+    lax.fori_loop(0, 16, spread, 0, unroll=SWAP_UNROLL)
 
 
 def y_group(index):
@@ -300,7 +324,7 @@
                 tile = mixed[pl.ds(pl.multiple_of(b * 16 + rh * 8, 8), 8), pl.ds(gh * 128, 128)]
                 dst[rh, pl.ds(pl.multiple_of(b * 16 + gh * 8, 8), 8), :] = swap8(tile)
         return 0
-    lax.fori_loop(0, 16, block, 0)
+    lax.fori_loop(0, 16, block, 0, unroll=SWAP_UNROLL)
 
 
 def greet_groups(barrier):
@@ -341,7 +365,7 @@
                 tile = r5[xh, pl.ds(ah * 128 + y, 8, stride=16), :]
                 lines[pl.ds(pl.multiple_of(y * 16 + xh * 8, 8), 8), pl.ds(ah * 128, 128)] = swap8(tile)
         return 0
-    lax.fori_loop(0, 16, gather, 0)
+    lax.fori_loop(0, 16, gather, 0, unroll=SWAP_UNROLL)
     values = product(split(lines[...]), cosine)
     first = gz == 0
     mine = jnp.where(first, values[:, :128], values[:, 128:])
@@ -368,23 +392,45 @@
     return pltpu.VMEM(shape, f32)
 
 
-def first_kernel(ids_ref, class_ref, cond_ref, table_ref, ext, row_ext, field, rows, send_sem, recv_sem):
+SCRATCH = dict(
+    ids=pltpu.VMEM((32, 16, 128), jnp.int32), classes=pltpu.VMEM((32, 16, 128), jnp.int32), cond=vmem(32, 16, 128),
+    forward=pltpu.VMEM((2, 256, 256), bf16), cosine=pltpu.VMEM((2, 256, 256), bf16),
+    eigen_x=vmem(256, 128), eigen_y=vmem(16, 256), eigen_z=vmem(16, 256), in_sem=DMA((8,)),
+    field=vmem(2, 32, 16, 128), rows=vmem(2, 2, 32, 128), ext=vmem(2, XE, YE, 256), row_ext=vmem(2, 2, 64, 256),
+    halo_send=DMA((20,)), halo_recv=DMA((20,)),
+    root=vmem(2, XE, 48, 128), gain=vmem(2, XE, YE, 128), keep=vmem(2, XE, YE, 128),
+    wa=vmem(3, 2, XE, 48, 128), wb=vmem(3, 2, XE, 48, 128), div=vmem(2, 256, 128), mixed=vmem(256, 256),
+    s1=vmem(2, 256, 128), r2=vmem(2, 256, 128), s2=vmem(2, 256, 128), r3=vmem(2, 256, 128), s3=vmem(2, 256, 128),
+    r4=vmem(2, 256, 128), s4=vmem(2, 256, 128), r5=vmem(2, 256, 128), lines=vmem(256, 256),
+    own_out=vmem(256, 128), peer_out=vmem(256, 128),
+    send_sem=DMA((4, 16)), recv_sem=DMA((4, 16)), last_send=DMA(()), last_recv=DMA(()),
+)
+
+
+def whole_kernel(ids_in, class_in, cond_in, forward_in, cosine_in, eigen_x_in, eigen_y_in, eigen_z_in, table_ref, normals_ref, out_ref, *scratch):
+    s = dict(zip(SCRATCH, scratch))
+    loads = [pltpu.make_async_copy(src, dst, s["in_sem"].at[k]) for k, (src, dst) in enumerate([
+        (ids_in, s["ids"]), (class_in, s["classes"]), (cond_in, s["cond"]), (forward_in, s["forward"]), (cosine_in, s["cosine"]),
+        (eigen_x_in, s["eigen_x"]), (eigen_y_in, s["eigen_y"]), (eigen_z_in, s["eigen_z"])])]
+    for load in loads:
+        load.start()
     barrier = pltpu.get_barrier_semaphore()
-    count = greet_halo(barrier)
-    fill_field(ids_ref, class_ref, cond_ref, table_ref, field, rows)
+    count = greet_halo(barrier) + greet_groups(barrier)
+    for load in loads[:3]:
+        load.wait()
+    fill_field(s["ids"], s["classes"], s["cond"], table_ref, s["field"], s["rows"])
     pl.semaphore_wait(barrier, count)
-    copies = halo_copies(field, rows, ext, row_ext, send_sem, recv_sem)
+    copies = halo_copies(s["field"], s["rows"], s["ext"], s["row_ext"], s["halo_send"], s["halo_recv"])
     for copy in copies:
         copy.start()
+    for load in loads[3:]:
+        load.wait()
     for copy in copies:
         copy.wait()
-
-
-def third_kernel(s1, *rest):
-    barrier = pltpu.get_barrier_semaphore()
-    count = greet_groups(barrier)
-    pl.semaphore_wait(barrier, count)
-    solve_part(s1, *rest)
+    heat_part(normals_ref, s["ext"], s["row_ext"], s["forward"], s["s1"], s["root"], s["gain"], s["keep"], s["wa"], s["wb"], s["div"], s["mixed"])
+    solve_part(s["s1"], s["forward"], s["cosine"], s["eigen_x"], s["eigen_y"], s["eigen_z"], out_ref, s["r2"], s["s2"], s["r3"], s["s3"],
+               s["r4"], s["s4"], s["r5"], s["lines"], s["own_out"], s["peer_out"], s["mixed"],
+               s["send_sem"], s["recv_sem"], s["last_send"], s["last_recv"])
 
 
 def per_device(surface_ids, class_map, conductivity, normals, class_table):
@@ -394,29 +440,13 @@
     eigen_x = jnp.asarray(np.repeat(eigen[:, None], 128, axis=1))
     eigen_y = jnp.asarray(np.repeat(eigen.reshape(16, 16), 16, axis=1))
     eigen_z = jnp.asarray(np.tile(eigen.reshape(16, 16), (1, 16)))
-    ext, row_ext = pl.pallas_call(
-        first_kernel,
-        out_shape=(jax.ShapeDtypeStruct((2, XE, YE, 256), f32), jax.ShapeDtypeStruct((2, 2, 64, 256), f32)),
-        in_specs=[VM, VM, VM, SM], out_specs=(VM, VM),
-        scratch_shapes=[vmem(2, 32, 16, 128), vmem(2, 2, 32, 128), DMA((20,)), DMA((20,))],
+    out = pl.pallas_call(
+        whole_kernel,
+        out_shape=jax.ShapeDtypeStruct((512, 128), f32),
+        in_specs=[pl.BlockSpec(memory_space=pl.ANY)] * 8 + [SM, VM], out_specs=VM,
+        scratch_shapes=list(SCRATCH.values()),
         compiler_params=pltpu.CompilerParams(collective_id=0, has_side_effects=True, vmem_limit_bytes=LIMIT),
-    )(surface_ids, class_map, conductivity, class_table)
-    s1 = pl.pallas_call(
-        heat_part,
-        out_shape=jax.ShapeDtypeStruct((2, 256, 128), f32),
-        in_specs=[VM, VM, VM, VM], out_specs=VM,
-        scratch_shapes=[vmem(XE, YE, 256), vmem(XE, YE, 256), vmem(XE, YE, 256), vmem(3, XE, YE, 256), vmem(3, XE, YE, 256),
-                        vmem(2, 64, 256), vmem(2, 3, 64, 256), vmem(2, 256, 128), vmem(256, 256)],
-        compiler_params=pltpu.CompilerParams(vmem_limit_bytes=LIMIT),
-    )(normals, ext, row_ext, forward_pair)
-    out = pl.pallas_call(
-        third_kernel,
-        out_shape=jax.ShapeDtypeStruct((512, 128), f32),
-        in_specs=[VM] * 6, out_specs=VM,
-        scratch_shapes=[vmem(2, 256, 128) for _ in range(7)] + [vmem(256, 256), vmem(256, 128), vmem(256, 128), vmem(256, 256),
-                        DMA((4, 16)), DMA((4, 16)), DMA(()), DMA(())],
-        compiler_params=pltpu.CompilerParams(collective_id=1, has_side_effects=True, vmem_limit_bytes=LIMIT),
-    )(s1, forward_pair, cosine_pair, eigen_x, eigen_y, eigen_z)
+    )(surface_ids, class_map, conductivity, forward_pair, cosine_pair, eigen_x, eigen_y, eigen_z, class_table, normals)
     return out.reshape(32, 16, 128)
 
 

time: 127 us -> 100 us (0.79)
  Pallas kernels: 121 us -> 90.9 us
  local copies, waits for them, and re-layouts: 5.9 us -> 9.13 us
    pallas_call x3 -> x1, Pallas kernels: 121 us -> 90.9 us  [per_device(): pl.pallas_call(whole_kernel, out_shape=jax.ShapeDtypeStruct((512, 128), f...]
    unnamed x21, local copies, waits for them, and re-layouts: 5.9 us -> 9.13 us
where the time goes in v2:
time: 100 us
  Pallas kernels  90.9 us (91%)
  local copies, waits for them, and re-layouts  9.13 us (9%)
    pallas_call x1, Pallas kernels, per_device(): pl.pallas_call(whole_kernel, out_shape=jax.ShapeDtypeStruct((512, 128), f...  90.9 us
    unnamed x21, local copies, waits for them, and re-layouts  9.13 us

profile of v2, /device:TPU:1, one launch (start us, length us, event | category | flops | bytes accessed | tf_op | source)
XLA Modules:
  0.0 100.0 jit_solution(12429969424342159516)
XLA Ops:
  0.0 0.0 copy-start
  0.0 0.9 copy-done
  1.0 0.0 copy-start.1
  1.0 0.9 copy-done.1
  1.9 0.0 copy-start.2
  1.9 0.9 copy-done.2
  2.9 0.0 copy-start.3
  2.9 0.9 copy-done.3
  3.8 0.0 copy-start.4
  3.8 0.9 copy-done.4
  4.8 0.0 copy-start.5
  4.8 0.9 copy-done.5
  5.7 0.0 copy-start.6
  5.7 0.7 copy-done.6
  6.4 0.0 copy-start.7
  6.4 0.7 copy-done.7
  7.1 0.0 copy-start.8
  7.1 0.7 copy-done.8
  7.8 0.0 copy-start.9
  7.8 0.7 copy-done.9
  8.4 90.9 %shard_map.100 = f32[512,128]{1,0:T(8,128)S(1)} custom-call(s32[32,16,128]{2,1,0:T(8,128)S(1)} %copy-done, s32[32,16,128]{2,1,0:T(8,128)S(1)} %copy-done.1, f32[32,16,128]{2,1,0:T(8,128)S(1)} %copy-done.2, bf16[2,256,256]{2,1,0:T(8,128)(2,1)S(1)} %copy-done.3, bf16[2,256,256]{2,1,0:T(8,128)(2,1)S(1)} %copy-done.4, f32[256,128]{1,0:T(8,128)S(1)} %copy-done.5, ...), custom_call_target="tpu_custom_call" | custom-call | tf_op jit(solution)/shard_map/pallas_call | solution.py:443
  99.3 0.7 copy.12
Async XLA Ops:
  0.0 0.9 copy-start
  1.0 0.9 copy-start.1
  1.9 0.9 copy-start.2
  2.9 0.9 copy-start.3
  3.8 0.9 copy-start.4
  4.8 0.9 copy-start.5
  5.7 0.7 copy-start.6
  6.4 0.7 copy-start.7
  7.1 0.7 copy-start.8
  7.8 0.7 copy-start.9

commit v3 on v2

--- a/solution.py
+++ b/solution.py
@@ -64,36 +64,53 @@
     return tile
 
 
+BOUNDS = (0, 9, 17, 25, 34)
+CHUNKS = ((0, 1), (2,), (3,))
+
+
 def halo_copies(field, rows, ext, row_ext, send_sem, recv_sem):
     gx, gy, gz = lax.axis_index("gx"), lax.axis_index("gy"), lax.axis_index("gz")
     lanes = pl.ds(pl.multiple_of(gz * 128, 128), 128)
-    copies = []
-    for dy in (1, -1, 0):
-        src_rows = {1: pl.ds(8, 8), -1: pl.ds(0, 8), 0: pl.ds(0, 16)}[dy]
-        dst_rows = {1: pl.ds(0, 8), -1: pl.ds(24, 8), 0: pl.ds(8, 16)}[dy]
-        to_y = lax.rem(gy + dy + 16, 16)
+    copies = {}
+
+    def remote(key, src, dst, x, y, core):
+        slot = len(copies)
+        copies[key] = pltpu.make_async_remote_copy(
+            src, dst, send_sem.at[slot], recv_sem.at[slot], device_id=(x, y, core), device_id_type=MESH)
+
+    def face(piece):
+        start, size = BOUNDS[piece], BOUNDS[piece + 1] - BOUNDS[piece]
+        for dy in (1, -1):
+            src_rows, dst_rows = (pl.ds(8, 8), pl.ds(0, 8)) if dy == 1 else (pl.ds(0, 8), pl.ds(24, 8))
+            for other in (0, 1):
+                core = 1 - gz if other else gz
+                if start == 0:
+                    first, x = 23 - 16 * core, lax.rem(gx + 1 - core, 8)
+                elif start >= 25:
+                    first, x = start - 9 - 16 * core, lax.rem(gx - core + 8, 8)
+                else:
+                    first, x = start - 9 + 16 * core, gx
+                remote(("face", piece, dy, other), field.at[:, pl.ds(first, size), src_rows, :],
+                       ext.at[:, pl.ds(start, size), dst_rows, lanes], x, lax.rem(gy + dy + 16, 16), core)
+
+    face(0)
+    face(1)
+    for other in (1, 0):
+        core = 1 - gz if other else gz
+        remote(("edge", other), field.at[:, pl.ds(23 * (1 - core), 9)], ext.at[:, pl.ds(25 * core, 9), pl.ds(8, 16), lanes],
+               lax.rem(gx + 1 - 2 * core + 8, 8), gy, core)
+        src, dst = field.at[:, pl.ds(7 * core, 25)], ext.at[:, pl.ds(9 * (1 - core), 25), pl.ds(8, 16), lanes]
+        if other:
+            remote(("block", 1), src, dst, gx, gy, core)
+        else:
+            copies["own"] = pltpu.make_async_copy(src, dst, recv_sem.at[len(copies)])
+    for side, dy in ((0, 1), (1, -1)):
         for other in (0, 1):
             core = 1 - gz if other else gz
-            to_x = lax.rem(gx + 1 - 2 * core + 8, 8)
-            parts = [
-                (field.at[:, pl.ds(7 * core, 25), src_rows, :], ext.at[:, pl.ds(9 * (1 - core), 25), dst_rows, lanes], gx),
-                (field.at[:, pl.ds(23 * (1 - core), 9), src_rows, :], ext.at[:, pl.ds(25 * core, 9), dst_rows, lanes], to_x),
-            ]
-            if dy:
-                side = 0 if dy == 1 else 1
-                parts += [
-                    (rows.at[side], row_ext.at[side, :, pl.ds(16, 32), lanes], gx),
-                    (rows.at[side, :, pl.ds(pl.multiple_of(16 * (1 - core), 16), 16), :],
-                     row_ext.at[side, :, pl.ds(pl.multiple_of(48 * core, 16), 16), lanes], to_x),
-                ]
-            for index, (src, dst, x) in enumerate(parts):
-                slot = len(copies)
-                if dy == 0 and other == 0 and index == 0:
-                    copies.append(pltpu.make_async_copy(src, dst, recv_sem.at[slot]))
-                else:
-                    copies.append(pltpu.make_async_remote_copy(
-                        src, dst, send_sem.at[slot], recv_sem.at[slot],
-                        device_id=(x, to_y, core), device_id_type=MESH))
+            remote(("row", side, other), rows.at[side, :, pl.ds(pl.multiple_of(16 * core, 16), 16), :],
+                   row_ext.at[side, :, :, lanes], gx, lax.rem(gy + dy + 16, 16), core)
+    for piece in range(2, len(BOUNDS) - 1):
+        face(piece)
     return copies
 
 
@@ -181,7 +198,7 @@
     return center, total
 
 
-def heat_part(normals_ref, ext, row_ext, forward_ref, out_ref, root, gain, keep, wa, wb, div, mixed):
+def heat_part(normals_ref, copies, ext, row_ext, forward_ref, out_ref, root, gain, keep, wa, wb, div, mixed):
     gx, gy, gz = lax.axis_index("gx"), lax.axis_index("gy"), lax.axis_index("gz")
     x0 = gx * 32 + gz * 16
     y0 = gy * 16
@@ -189,42 +206,57 @@
     def tables(r):
         return [tuple(jnp.broadcast_to(normals_ref[j:j + 1, h * 128:(h + 1) * 128], (r, 128)) for h in range(2)) for j in range(3)]
 
-    y_of = lax.broadcasted_iota(jnp.int32, (YE, 128), 0) + (y0 - 8)
-    y_inside = jnp.logical_and(y_of >= 0, y_of < N)
-
-    def start(i, _):
+    def sources(i, parts):
         x = x0 - HALO + i
         x_in = jnp.logical_and(x >= 0, x < N)
-        inside = jnp.logical_and(y_inside, x_in)
-        r = i + 7 + 16 * gz
         done = []
+        for first, count in parts:
+            y = lax.broadcasted_iota(jnp.int32, (count, 128), 0) + (y0 - 8 + first)
+            inside = jnp.logical_and(jnp.logical_and(y >= 0, y < N), x_in)
+            for h in range(2):
+                lanes = pl.ds(h * 128, 128)
+                value = jnp.where(inside, ext[0, i, pl.ds(first, count), lanes], 0.0)
+                found = lookup(ext[1, i, pl.ds(first, count), lanes], tables(count))
+                done.append((h, pl.ds(8 + first, count), value, [found[j] * value for j in range(3)]))
+        for h, where, value, w in done:
+            root[h, i, where] = value
+            for j in range(3):
+                wa[j, h, i, where] = w[j]
+
+    zero = jnp.zeros((XE, 128), f32)
+    for row in (7, 40):
         for h in range(2):
-            lanes = pl.ds(h * 128, 128)
-            value = jnp.where(inside, ext[0, i, :, lanes], 0.0)
-            found = lookup(ext[1, i, :, lanes], tables(YE))
-            done.append((value, [found[j] * value for j in range(3)]))
-        for h in range(2):
-            root[h, i, BODY] = done[h][0]
+            root[h, :, row, :] = zero
             for j in range(3):
-                wa[j, h, i, BODY] = done[h][1][j]
-        return 0
-    lax.fori_loop(0, XE, start, 0, unroll=LOOKUP_UNROLL)
-
-    x_of = lax.broadcasted_iota(jnp.int32, (40, 128), 0) + (x0 - HALO)
-    x_inside = jnp.logical_and(x_of >= 0, x_of < N)
-    wide = pl.ds(pl.multiple_of(16 * gz, 8), 48)
+                wa[j, h, :, row, :] = zero
+                wb[j, h, :, row, :] = zero
+
+    for key in (("block", 1), ("edge", 1), ("edge", 0), "own"):
+        copies[key].wait()
+
+    def middle(i, _):
+        sources(i, [(8, 16)])
+        return 0
+    lax.fori_loop(0, XE, middle, 0, unroll=LOOKUP_UNROLL)
+
+    for side, dy in ((0, 1), (1, -1)):
+        for other in (0, 1):
+            copies[("row", side, other)].wait()
     for side in range(2):
         y = y0 - 9 if side == 0 else y0 + 24
-        inside = jnp.logical_and(x_inside, jnp.logical_and(y >= 0, y < N))
+        y_in = jnp.logical_and(y >= 0, y < N)
         row = 7 if side == 0 else 40
         for h in range(2):
             lanes = pl.ds(h * 128, 128)
-            value = jnp.where(inside, row_ext[side, 0, wide, lanes][7:47], 0.0)
-            found = lookup(row_ext[side, 1, wide, lanes][7:47], tables(40))
-            root[h, :, row, :] = value[:XE]
+            value = jnp.where(y_in, row_ext[side, 0, :, lanes], 0.0)
+            found = lookup(row_ext[side, 1, :, lanes], tables(16))
+            root[h, pl.ds(9, 16), row, :] = value
             for j in range(3):
-                wa[j, h, :, row, :] = (found[j] * value)[:XE]
-                wb[j, h, :, row, :] = jnp.zeros((XE, 128), f32)
+                wa[j, h, pl.ds(9, 16), row, :] = found[j] * value
+
+    def sides(i, _):
+        sources(i, [(0, 8), (24, 8)])
+        return 0
 
     def coefficients(i, _):
         center, total = neighbours(root, (), i)
@@ -232,12 +264,9 @@
             keep[h, i] = 1.0 - time_step * center[h] * total[h]
             gain[h, i] = time_step * center[h] * center[h]
         return 0
-    lax.fori_loop(1, XE - 1, coefficients, 0, unroll=UNROLL)
-
-    for step in range(1, STEPS + 1):
-        src, dst = (wa, wb) if step % 2 else (wb, wa)
-
-        def plane(i, _, src=src, dst=dst):
+
+    def plane(src, dst):
+        def body(i, _):
             done = []
             for j in range(3):
                 center, total = neighbours(src, (j,), i)
@@ -246,7 +275,7 @@
             for j, h, value in done:
                 dst[j, h, i, BODY] = value
             return 0
-        lax.fori_loop(step, XE - step, plane, 0, unroll=UNROLL)
+        return body
 
     def unit(i, _):
         for h in range(2):
@@ -257,7 +286,36 @@
             for j in range(3):
                 wb[j, h, i, BODY] = w[j] * scale
         return 0
-    lax.fori_loop(STEPS, XE - STEPS, unit, 0, unroll=UNROLL)
+
+    before = 0
+    for pieces in CHUNKS:
+        reach = BOUNDS[pieces[-1] + 1]
+        for piece in pieces:
+            for dy in (1, -1):
+                for other in (0, 1):
+                    copies[("face", piece, dy, other)].wait()
+        lax.fori_loop(before, reach, sides, 0, unroll=LOOKUP_UNROLL)
+        lax.fori_loop(max(1, before - 1), reach - 1, coefficients, 0, unroll=UNROLL)
+        if before < 2 * STEPS + 1:
+            for step in range(1, STEPS + 1):
+                first, end = max(step, before - step), reach - step
+                src, dst = (wa, wb) if step % 2 else (wb, wa)
+                if first < end:
+                    lax.fori_loop(first, end, plane(src, dst), 0, unroll=min(UNROLL, end - first))
+        else:
+            def pair(p, _, before=before, reach=reach):
+                for odd, src, dst in ((1, wa, wb), (2, wb, wa)):
+                    first = before - odd - 2 * p
+                    body = plane(src, dst)
+                    for k in range(reach - before):
+                        body(first + k, 0)
+                return 0
+            lax.fori_loop(0, STEPS // 2, pair, 0)
+        first = max(STEPS, before - STEPS - 1)
+        end = XE - STEPS if reach == XE else reach - STEPS - 1
+        if first < end:
+            lax.fori_loop(first, end, unit, 0, unroll=min(UNROLL, end - first))
+        before = reach
 
     def divergence(k, _):
         i = k + HALO
@@ -267,7 +325,7 @@
             part_y = wb[1, h, i, pl.ds(17, 16)] - wb[1, h, i, pl.ds(15, 16)]
             div[h, pl.ds(pl.multiple_of(k * 16, 16), 16), :] = part_x + part_y + part_z[h]
         return 0
-    lax.fori_loop(0, 16, divergence, 0, unroll=UNROLL)
+    lax.fori_loop(0, 16, divergence, 0, unroll=4)
 
     lines = jnp.concatenate(
         [jnp.concatenate([div[h, pl.ds(y, 16, stride=16), :] for y in range(16)], axis=0) for h in range(2)], axis=1)
@@ -385,7 +443,7 @@
 VM = pl.BlockSpec(memory_space=pltpu.VMEM)
 SM = pl.BlockSpec(memory_space=pltpu.SMEM)
 DMA = pltpu.SemaphoreType.DMA
-LIMIT = 48 * 1024 * 1024
+LIMIT = 62 * 1024 * 1024
 
 
 def vmem(*shape):
@@ -396,8 +454,8 @@
     ids=pltpu.VMEM((32, 16, 128), jnp.int32), classes=pltpu.VMEM((32, 16, 128), jnp.int32), cond=vmem(32, 16, 128),
     forward=pltpu.VMEM((2, 256, 256), bf16), cosine=pltpu.VMEM((2, 256, 256), bf16),
     eigen_x=vmem(256, 128), eigen_y=vmem(16, 256), eigen_z=vmem(16, 256), in_sem=DMA((8,)),
-    field=vmem(2, 32, 16, 128), rows=vmem(2, 2, 32, 128), ext=vmem(2, XE, YE, 256), row_ext=vmem(2, 2, 64, 256),
-    halo_send=DMA((20,)), halo_recv=DMA((20,)),
+    field=vmem(2, 32, 16, 128), rows=vmem(2, 2, 32, 128), ext=vmem(2, XE, YE, 256), row_ext=vmem(2, 2, 16, 256),
+    halo_send=DMA((40,)), halo_recv=DMA((40,)),
     root=vmem(2, XE, 48, 128), gain=vmem(2, XE, YE, 128), keep=vmem(2, XE, YE, 128),
     wa=vmem(3, 2, XE, 48, 128), wb=vmem(3, 2, XE, 48, 128), div=vmem(2, 256, 128), mixed=vmem(256, 256),
     s1=vmem(2, 256, 128), r2=vmem(2, 256, 128), s2=vmem(2, 256, 128), r3=vmem(2, 256, 128), s3=vmem(2, 256, 128),
@@ -421,13 +479,11 @@
     fill_field(s["ids"], s["classes"], s["cond"], table_ref, s["field"], s["rows"])
     pl.semaphore_wait(barrier, count)
     copies = halo_copies(s["field"], s["rows"], s["ext"], s["row_ext"], s["halo_send"], s["halo_recv"])
-    for copy in copies:
+    for copy in copies.values():
         copy.start()
     for load in loads[3:]:
         load.wait()
-    for copy in copies:
-        copy.wait()
-    heat_part(normals_ref, s["ext"], s["row_ext"], s["forward"], s["s1"], s["root"], s["gain"], s["keep"], s["wa"], s["wb"], s["div"], s["mixed"])
+    heat_part(normals_ref, copies, s["ext"], s["row_ext"], s["forward"], s["s1"], s["root"], s["gain"], s["keep"], s["wa"], s["wb"], s["div"], s["mixed"])
     solve_part(s["s1"], s["forward"], s["cosine"], s["eigen_x"], s["eigen_y"], s["eigen_z"], out_ref, s["r2"], s["s2"], s["r3"], s["s3"],
                s["r4"], s["s4"], s["r5"], s["lines"], s["own_out"], s["peer_out"], s["mixed"],
                s["send_sem"], s["recv_sem"], s["last_send"], s["last_recv"])
@@ -443,7 +499,7 @@
     out = pl.pallas_call(
         whole_kernel,
         out_shape=jax.ShapeDtypeStruct((512, 128), f32),
-        in_specs=[pl.BlockSpec(memory_space=pl.ANY)] * 8 + [SM, VM], out_specs=VM,
+        in_specs=[pl.BlockSpec(memory_space=pltpu.HBM)] * 8 + [SM, VM], out_specs=VM,
         scratch_shapes=list(SCRATCH.values()),
         compiler_params=pltpu.CompilerParams(collective_id=0, has_side_effects=True, vmem_limit_bytes=LIMIT),
     )(surface_ids, class_map, conductivity, forward_pair, cosine_pair, eigen_x, eigen_y, eigen_z, class_table, normals)

time: 100 us -> 83.5 us (0.83)
  Pallas kernels: 90.9 us -> 81.6 us
  local copies, waits for them, and re-layouts: 9.13 us -> 1.67 us
    pallas_call x1, Pallas kernels: 90.9 us -> 81.6 us  [per_device(): pl.pallas_call(whole_kernel, out_shape=jax.ShapeDtypeStruct((512, 128), f...]
    unnamed x21 -> x1, local copies, waits for them, and re-layouts: 9.13 us -> 1.67 us
where the time goes in v3:
time: 83.5 us; the launch traced here: 83.3 us
  Pallas kernels  81.6 us (98%)
  local copies, waits for them, and re-layouts  1.67 us (2%)
    pallas_call x1, Pallas kernels, per_device(): pl.pallas_call(whole_kernel, out_shape=jax.ShapeDtypeStruct((512, 128), f...  81.6 us
    unnamed x1, local copies, waits for them, and re-layouts  1.67 us

profile of v3, /device:TPU:1, one launch (start us, length us, event | category | flops | bytes accessed | tf_op | source)
XLA Modules:
  0.0 83.3 jit_solution(13980159522315167197)
XLA Ops:
  0.0 81.6 %shard_map.100 = f32[512,128]{1,0:T(8,128)} custom-call(s32[32,16,128]{2,1,0:T(8,128)} %ids_in.1, s32[32,16,128]{2,1,0:T(8,128)} %class_in.1, f32[32,16,128]{2,1,0:T(8,128)} %cond_in.1, bf16[2,256,256]{2,1,0:T(8,128)(2,1)} %constant.11.clone.forward_in, bf16[2,256,256]{2,1,0:T(8,128)(2,1)} %constant.10.clone.cosine_in, ...), custom_call_target="tpu_custom_call" | custom-call | tf_op jit(solution)/shard_map/pallas_call | solution.py:499
  81.7 1.7 %copy.12 = f32[32,16,128]{2,1,0:T(8,128)} copy(f32[32,16,128]{2,1,0:T(8,128)} %bitcast.1) | data formatting | bytes 524288

commit v4 on v3

v4 whole, which is shorter than its diff:
```python
import jax
import jax.numpy as jnp
import numpy as np
from jax import lax
from jax.experimental import pallas as pl
from jax.experimental.pallas import tpu as pltpu
from jax.sharding import PartitionSpec as P

N = 256
STEPS = 8
CLASSES = 4
HALO = STEPS + 1
XE = 16 + 2 * HALO
YE = 32
time_step = 0.08
norm_floor = 0.5
f32 = jnp.float32
bf16 = jnp.bfloat16
MESH = pl.DeviceIdType.MESH


def cosine_table():
    wave_number = np.arange(N, dtype=np.float32)[:, None]
    sample = np.arange(N, dtype=np.float32)[None, :]
    factor = np.where(wave_number == 0, np.sqrt(np.float32(1.0 / N)), np.sqrt(np.float32(2.0 / N)))
    angle = np.float32(np.pi) * wave_number * (np.float32(2.0) * sample + np.float32(1.0)) / np.float32(2.0 * N)
    return (factor * np.cos(angle)).astype(np.float32)


def eigen_values():
    wave_number = np.arange(N, dtype=np.float32)
    return (np.float32(2.0) - np.float32(2.0) * np.cos(np.float32(np.pi) * wave_number / np.float32(N))).astype(np.float32)


def halves(table):
    high = table.astype(jnp.bfloat16)
    low = (table - high.astype(np.float32)).astype(jnp.bfloat16)
    return np.stack([high, low])


def split(values):
    high = values.astype(bf16)
    return high, (values - high.astype(f32)).astype(bf16)


def product(left, right):
    dot = lambda a, b: jnp.dot(a, b, preferred_element_type=f32)
    return dot(left[0], right[0]) + (dot(left[1], right[0]) + dot(left[0], right[1]))


def swap8(tile):
    row = lax.broadcasted_iota(jnp.int32, (8, 128), 0)
    group = lax.broadcasted_iota(jnp.int32, (8, 128), 1) // 16
    for bit in (1, 2, 4):
        row_bit = (row // bit) % 2
        group_bit = (group // bit) % 2
        if bit == 4:
            other = pltpu.roll(pltpu.roll(tile, 4, 0), 64, 1)
        else:
            forth = pltpu.roll(pltpu.roll(tile, bit, 0), 128 - 16 * bit, 1)
            back = pltpu.roll(pltpu.roll(tile, 8 - bit, 0), 16 * bit, 1)
            other = jnp.where(row_bit == 1, forth, back)
        tile = jnp.where(row_bit == group_bit, tile, other)
    return tile


INNER = ((7, 9), (16, 9))
OUTER = ((0, 7), (25, 7))
MARCH = True


def halo_copies(field, rows, ext, row_ext, send_sem, recv_sem):
    gx, gy, gz = lax.axis_index("gx"), lax.axis_index("gy"), lax.axis_index("gz")
    lanes = pl.ds(pl.multiple_of(gz * 128, 128), 128)
    copies = {}

    def remote(key, src, dst, x, y, core):
        slot = len(copies)
        copies[key] = pltpu.make_async_remote_copy(
            src, dst, send_sem.at[slot], recv_sem.at[slot], device_id=(x, y, core), device_id_type=MESH)

    def next_y(dy):
        return lax.rem(gy + dy + 16, 16)

    def next_x(core):
        return lax.rem(gx + 1 - 2 * core + 8, 8)

    for first, size in INNER + OUTER:
        for dy in (1, -1):
            src_rows, dst_rows = (pl.ds(8, 8), pl.ds(0, 8)) if dy == 1 else (pl.ds(0, 8), pl.ds(24, 8))
            place = ext.at[:, pl.ds(9 + first, size), dst_rows, lanes]
            remote(("face", first, dy), field.at[:, pl.ds(first, size), src_rows, :], place, gx, next_y(dy), gz)
            if (first, size) in INNER:
                remote(("pass", first, dy), place, place, gx, gy, 1 - gz)
    for dy in (1, -1):
        dst_rows = pl.ds(0, 8) if dy == 1 else pl.ds(24, 8)
        place = ext.at[:, pl.ds(9 + 25 * (1 - gz), 7), dst_rows, lanes]
        remote(("pass", "outer", dy), place, place, gx, gy, 1 - gz)
        for other in (0, 1):
            core = 1 - gz if other else gz
            remote(("corner", other, dy), ext.at[:, pl.ds(9 + 23 * (1 - core), 9), dst_rows, lanes],
                   ext.at[:, pl.ds(41 * core, 9), dst_rows, lanes], next_x(core), gy, core)
    middle_rows = pl.ds(8, 16)
    for other in (1, 0):
        core = 1 - gz if other else gz
        remote(("edge", other), field.at[:, pl.ds(23 * (1 - core), 9)], ext.at[:, pl.ds(41 * core, 9), middle_rows, lanes],
               next_x(core), gy, core)
        src, dst = field.at[:, pl.ds(7 * core, 25)], ext.at[:, pl.ds(9 + 7 * core, 25), middle_rows, lanes]
        if other:
            remote(("block", 1), src, dst, gx, gy, core)
        else:
            copies["own"] = pltpu.make_async_copy(src, dst, recv_sem.at[len(copies)])
    for side, dy in ((0, 1), (1, -1)):
        for other in (0, 1):
            core = 1 - gz if other else gz
            remote(("row", side, other), rows.at[side, :, pl.ds(pl.multiple_of(16 * core, 16), 16), :],
                   row_ext.at[side, :, :, lanes], gx, next_y(dy), core)
    return copies


def start_all(copies, *kinds):
    for kind in kinds:
        for key, copy in copies.items():
            if key == kind or key[:len(kind)] == kind:
                copy.start()


def wait_all(copies, *kinds):
    for kind in kinds:
        for key, copy in copies.items():
            if key == kind or key[:len(kind)] == kind:
                copy.wait()


def greet_halo(barrier):
    gx, gy, gz = lax.axis_index("gx"), lax.axis_index("gy"), lax.axis_index("gz")
    from_x = lax.rem(gx + 2 * gz - 1 + 8, 8)
    others = [(gx, lax.rem(gy + dy + 16, 16), core) for dy in (1, -1) for core in (0, 1)]
    others += [(gx, gy, 1 - gz), (from_x, gy, 0), (from_x, gy, 1)]
    for other in others:
        pl.semaphore_signal(barrier, inc=1, device_id=other, device_id_type=MESH)
    return len(others)


def fill_field(ids_ref, class_ref, cond_ref, table_ref, field, rows):
    lane = lax.broadcasted_iota(jnp.int32, (16, 128), 1)
    odd_first = lax.axis_index("gz")
    order = 2 * (lane % 64) + jnp.where(lane < 64, odd_first, 1 - odd_first)

    def plane(i, _):
        classes = class_ref[i]
        value = jnp.full(classes.shape, table_ref[0], f32)
        for k in range(1, CLASSES):
            value = jnp.where(classes == k, table_ref[k], value)
        root = jnp.sqrt(value * cond_ref[i])
        field[0, i] = jnp.take_along_axis(root, order, axis=1)
        field[1, i] = jnp.take_along_axis(ids_ref[i].astype(f32), order, axis=1)
        return 0
    lax.fori_loop(0, 32, plane, 0, unroll=4)
    for which in range(2):
        rows[0, which] = field[which, :, 7, :]
        rows[1, which] = field[which, :, 8, :]


def even_odd(first, second):
    low = lax.broadcasted_iota(jnp.int32, first.shape, 1) < 64
    return jnp.where(low, first, second), pltpu.roll(jnp.where(low, second, first), 64, 1)


def lookup(ids_float, tables):
    index = ids_float.astype(jnp.int32) - 1
    low = jnp.bitwise_and(index, 127)
    found = []
    for first, second in tables:
        a = jnp.take_along_axis(first, low, axis=1)
        b = jnp.take_along_axis(second, low, axis=1)
        found.append(jnp.where(index < 0, 0.0, jnp.where(index < 128, a, b)))
    return found


SWAP_UNROLL = 16
UNROLL = 6
UNALIGNED = True
LOOKUP_UNROLL = 4


def z_sides(even, odd):
    lane = lax.broadcasted_iota(jnp.int32, even.shape, 1)
    return jnp.where(lane == 0, 0.0, pltpu.roll(odd, 1, 1)), jnp.where(lane == 127, 0.0, pltpu.roll(even, 127, 1))


def z_sum(even, odd):
    before, after = z_sides(even, odd)
    return before + odd, even + after


def z_difference(even, odd):
    before, after = z_sides(even, odd)
    return odd - before, after - even


BODY = pl.ds(8, YE)


def neighbours(ref, lead, i):
    center = [ref[lead + (h, i, BODY)] for h in range(2)]
    sides = z_sum(*center)
    total = []
    for h in range(2):
        if UNALIGNED:
            y = ref[lead + (h, i, pl.ds(7, YE))] + ref[lead + (h, i, pl.ds(9, YE))]
        else:
            y = pltpu.roll(center[h], 1, 0) + pltpu.roll(center[h], YE - 1, 0)
        x = ref[lead + (h, i - 1, BODY)] + ref[lead + (h, i + 1, BODY)]
        total.append((x + y) + sides[h])
    return center, total


def heat_part(normals_ref, copies, ext, row_ext, forward_ref, out_ref, root, gain, keep, wa, wb, row_w, div, mixed):
    gx, gy, gz = lax.axis_index("gx"), lax.axis_index("gy"), lax.axis_index("gz")
    y0 = gy * 16

    def tables(r):
        return [tuple(jnp.broadcast_to(normals_ref[j:j + 1, h * 128:(h + 1) * 128], (r, 128)) for h in range(2)) for j in range(3)]

    def sources(m, parts):
        p = 33 - m + gz * (2 * m - 17)
        x = gx * 32 - HALO + p
        x_in = jnp.logical_and(x >= 0, x < N)
        done = []
        for first, count in parts:
            y = lax.broadcasted_iota(jnp.int32, (count, 128), 0) + (y0 - 8 + first)
            inside = jnp.logical_and(jnp.logical_and(y >= 0, y < N), x_in)
            both = [even_odd(*[ext[a, p, pl.ds(first, count), pl.ds(c * 128, 128)] for c in range(2)]) for a in range(2)]
            for h in range(2):
                value = jnp.where(inside, both[0][h], 0.0)
                found = lookup(both[1][h], tables(count))
                done.append((h, pl.ds(8 + first, count), value, [found[j] * value for j in range(3)]))
        for h, where, value, w in done:
            root[h, m, where] = value
            for j in range(3):
                wa[j, h, m, where] = w[j]

    def middle(m, _):
        sources(m, [(8, 16)])
        return 0

    def sides(m, _):
        sources(m, [(0, 8), (24, 8)])
        return 0

    def coefficients(m, _):
        center, total = neighbours(root, (), m)
        for h in range(2):
            keep[h, m] = 1.0 - time_step * center[h] * total[h]
            gain[h, m] = time_step * center[h] * center[h]
        return 0

    def march(src, dst, first, count):
        if not MARCH:
            for k in range(count):
                m = first + k
                done = []
                for j in range(3):
                    center, total = neighbours(src, (j,), m)
                    for h in range(2):
                        done.append((j, h, keep[h, m] * center[h] + gain[h, m] * total[h]))
                for j, h, value in done:
                    dst[j, h, m, BODY] = value
            return
        pairs = [(j, h) for j in range(3) for h in range(2)]
        for r in range(YE // 8):
            here, above, below = pl.ds(8 + 8 * r, 8), pl.ds(7 + 8 * r, 8), pl.ds(9 + 8 * r, 8)
            last = {q: src[q + (first - 1, here)] for q in pairs}
            now = {q: src[q + (first, here)] for q in pairs}
            for k in range(count):
                m = first + k
                coming = {q: src[q + (m + 1, here)] for q in pairs}
                scale = [(keep[h, m, pl.ds(8 * r, 8)], gain[h, m, pl.ds(8 * r, 8)]) for h in range(2)]
                done = {}
                for j in range(3):
                    z = z_sum(now[j, 0], now[j, 1])
                    for h in range(2):
                        q = (j, h)
                        y = src[q + (m, above)] + src[q + (m, below)]
                        done[q] = scale[h][0] * now[q] + scale[h][1] * ((last[q] + coming[q]) + (y + z[h]))
                for q in pairs:
                    dst[q + (m, here)] = done[q]
                last, now = now, coming

    def unit(m, _):
        for h in range(2):
            w = [wa[j, h, m, BODY] for j in range(3)]
            size = jnp.sqrt(w[0] * w[0] + w[1] * w[1] + w[2] * w[2])
            floor = jnp.maximum(jnp.maximum(size, norm_floor * root[h, m, BODY]), 1e-30)
            scale = 0.5 / floor
            for j in range(3):
                wb[j, h, m, BODY] = w[j] * scale
        return 0

    def looked_up(body, first, end):
        lax.fori_loop(first, end, body, 0, unroll=LOOKUP_UNROLL)

    zero = jnp.zeros((XE, 128), f32)
    for row in (7, 40):
        for h in range(2):
            root[h, :, row, :] = zero
            for j in range(3):
                wa[j, h, :, row, :] = zero
                wb[j, h, :, row, :] = zero

    wait_all(copies, "own", ("block",))
    looked_up(middle, 0, 12)
    for first, _ in INNER:
        for dy in (1, -1):
            copies["face", first, dy].wait()
            copies["pass", first, dy].start()
    looked_up(middle, 12, 25)
    wait_all(copies, ("row",))
    for side in range(2):
        y = y0 - 9 if side == 0 else y0 + 24
        y_in = jnp.logical_and(y >= 0, y < N)
        both = [even_odd(*[row_ext[side, a, :, pl.ds(c * 128, 128)] for c in range(2)]) for a in range(2)]
        for h in range(2):
            value = jnp.where(y_in, both[0][h], 0.0)
            found = lookup(both[1][h], tables(16))
            row_w[side, h, 3] = value
            for j in range(3):
                row_w[side, h, j] = found[j] * value

    def outer_row(m, _):
        k = 24 - m + gz * (2 * m - 33)
        for side, row in ((0, 7), (1, 40)):
            for h in range(2):
                root[h, m, pl.ds(row, 1)] = row_w[side, h, 3, pl.ds(k, 1)]
                for j in range(3):
                    wa[j, h, m, pl.ds(row, 1)] = row_w[side, h, j, pl.ds(k, 1)]
        return 0
    lax.fori_loop(9, 25, outer_row, 0, unroll=4)

    for before, reach in ((0, 18), (18, 25), (25, XE)):
        if before == 0:
            wait_all(copies, ("pass", INNER[0][0]), ("pass", INNER[1][0]))
        elif before == 18:
            wait_all(copies, ("pass", "outer"))
        else:
            wait_all(copies, ("edge",), ("corner",))
            looked_up(middle, before, reach)
        looked_up(sides, before, reach)
        lax.fori_loop(max(1, before - 1), reach - 1, coefficients, 0, unroll=UNROLL)
        if before == 0:
            for first, _ in OUTER:
                for dy in (1, -1):
                    copies["face", first, dy].wait()
            start_all(copies, ("pass", "outer"), ("corner",))
            for step in range(1, STEPS + 1):
                src, dst = (wa, wb) if step % 2 else (wb, wa)
                march(src, dst, step, reach - 2 * step)
        else:
            def pair(p, _, before=before, reach=reach):
                for odd, src, dst in ((1, wa, wb), (2, wb, wa)):
                    march(src, dst, before - odd - 2 * p, reach - before)
                return 0
            lax.fori_loop(0, STEPS // 2, pair, 0)
        first = max(STEPS, before - STEPS - 1)
        end = XE - STEPS if reach == XE else reach - STEPS - 1
        lax.fori_loop(first, end, unit, 0, unroll=min(UNROLL, end - first))

    sign = (2 * gz - 1).astype(f32)

    def divergence(k, _):
        m = 24 - k + gz * (2 * k - 15)
        part_z = z_difference(*[wb[2, h, m, pl.ds(16, 16)] for h in range(2)])
        for h in range(2):
            part_x = sign * (wb[0, h, m + 1, pl.ds(16, 16)] - wb[0, h, m - 1, pl.ds(16, 16)])
            part_y = wb[1, h, m, pl.ds(17, 16)] - wb[1, h, m, pl.ds(15, 16)]
            div[h, pl.ds(pl.multiple_of(k * 16, 16), 16), :] = part_x + part_y + part_z[h]
        return 0
    lax.fori_loop(0, 16, divergence, 0, unroll=4)

    lines = jnp.concatenate(
        [jnp.concatenate([div[h, pl.ds(y, 16, stride=16), :] for y in range(16)], axis=0) for h in range(2)], axis=1)
    mixed[...] = product(split(lines), (forward_ref[0], forward_ref[1]))

    def spread(y, _):
        for xh in range(2):
            for ah in range(2):
                tile = mixed[pl.ds(pl.multiple_of(y * 16 + xh * 8, 8), 8), pl.ds(ah * 128, 128)]
                out_ref[xh, pl.ds(ah * 128 + y, 8, stride=16), :] = swap8(tile)
        return 0
    lax.fori_loop(0, 16, spread, 0, unroll=SWAP_UNROLL)


def y_group(index):
    return (lax.axis_index("gx"), index, lax.axis_index("gz"))


def x_group(index):
    return (index // 2, lax.axis_index("gy"), index % 2)


def exchange(src, dst, me, where, send_sem, recv_sem):
    def copy(d):
        to = lax.rem(me + d, 16)
        return pltpu.make_async_remote_copy(
            src.at[:, pl.ds(pl.multiple_of(to * 16, 16), 16), :],
            dst.at[:, pl.ds(pl.multiple_of(me * 16, 16), 16), :],
            send_sem.at[d], recv_sem.at[d], device_id=where(to), device_id_type=MESH)

    for d in (8, 7, 9, 6, 10, 5, 11, 4, 12, 3, 13, 2, 14, 1, 15):
        copy(d).start()
    own = pl.ds(pl.multiple_of(me * 16, 16), 16)
    dst[:, own, :] = src[:, own, :]

    for d in range(1, 16):
        copy(d).wait()


def whole(ref):
    return jnp.concatenate([ref[0], ref[1]], axis=1)


def turn(values, mixed, dst):
    mixed[...] = values

    def block(b, _):
        for rh in range(2):
            for gh in range(2):
                tile = mixed[pl.ds(pl.multiple_of(b * 16 + rh * 8, 8), 8), pl.ds(gh * 128, 128)]
                dst[rh, pl.ds(pl.multiple_of(b * 16 + gh * 8, 8), 8), :] = swap8(tile)
        return 0
    lax.fori_loop(0, 16, block, 0, unroll=SWAP_UNROLL)


def greet_groups(barrier):
    gx, gy, gz = lax.axis_index("gx"), lax.axis_index("gy"), lax.axis_index("gz")
    group = gx * 2 + gz

    def greet(d, _):
        pl.semaphore_signal(barrier, inc=1, device_id=y_group(lax.rem(gy + d, 16)), device_id_type=MESH)
        pl.semaphore_signal(barrier, inc=1, device_id=x_group(lax.rem(group + d, 16)), device_id_type=MESH)
        return 0
    lax.fori_loop(1, 16, greet, 0)
    return 30


def solve_part(s1, forward_ref, cosine_ref, eigen_x, eigen_y, eigen_z, out_ref, r2, s2, r3, s3, r4, s4, r5, lines, own_out, peer_out, mixed,
               send_sem, recv_sem, last_send, last_recv):
    gx, gy, gz = lax.axis_index("gx"), lax.axis_index("gy"), lax.axis_index("gz")
    group = gx * 2 + gz
    cosine = (cosine_ref[0], cosine_ref[1])
    forward = (forward_ref[0], forward_ref[1])
    exchange(s1, r2, gy, y_group, send_sem.at[0], recv_sem.at[0])
    turn(product(cosine, split(whole(r2))), mixed, s2)
    exchange(s2, r3, group, x_group, send_sem.at[1], recv_sem.at[1])
    spectrum = product(cosine, split(whole(r3)))
    rest = eigen_y[pl.ds(group, 1), :] + eigen_z[pl.ds(gy, 1), :]
    eigen = jnp.concatenate([eigen_x[...], eigen_x[...]], axis=1)
    solved = -spectrum / (eigen + rest + 4.0 / (N * N))
    turn(product(forward, split(solved)), mixed, s3)
    exchange(s3, r4, group, x_group, send_sem.at[2], recv_sem.at[2])
    values = product(forward, split(whole(r4)))
    for h in range(2):
        s4[h] = values[:, h * 128:(h + 1) * 128]
    exchange(s4, r5, gy, y_group, send_sem.at[3], recv_sem.at[3])

    def gather(y, _):
        for xh in range(2):
            for ah in range(2):
                tile = r5[xh, pl.ds(ah * 128 + y, 8, stride=16), :]
                lines[pl.ds(pl.multiple_of(y * 16 + xh * 8, 8), 8), pl.ds(ah * 128, 128)] = swap8(tile)
        return 0
    lax.fori_loop(0, 16, gather, 0, unroll=SWAP_UNROLL)
    values = product(split(lines[...]), cosine)
    first = gz == 0
    mine = jnp.where(first, values[:, :128], values[:, 128:])
    theirs = jnp.where(first, values[:, 128:], values[:, :128])
    for y in range(16):
        peer_out[pl.ds(y, 16, stride=16), :] = theirs[y * 16:(y + 1) * 16]
    rows = pl.ds(pl.multiple_of(gz * 256, 256), 256)
    copy = pltpu.make_async_remote_copy(
        peer_out, out_ref.at[rows, :], last_send, last_recv, device_id=(gx, gy, 1 - gz), device_id_type=MESH)
    copy.start()
    for y in range(16):
        own_out[pl.ds(y, 16, stride=16), :] = mine[y * 16:(y + 1) * 16]
    out_ref[rows, :] = own_out[...]
    copy.wait()


VM = pl.BlockSpec(memory_space=pltpu.VMEM)
SM = pl.BlockSpec(memory_space=pltpu.SMEM)
DMA = pltpu.SemaphoreType.DMA
LIMIT = 62 * 1024 * 1024


def vmem(*shape):
    return pltpu.VMEM(shape, f32)


SCRATCH = dict(
    ids=pltpu.VMEM((32, 16, 128), jnp.int32), classes=pltpu.VMEM((32, 16, 128), jnp.int32), cond=vmem(32, 16, 128),
    first=pltpu.VMEM((2, 256, 256), bf16), forward=pltpu.VMEM((2, 256, 256), bf16), cosine=pltpu.VMEM((2, 256, 256), bf16),
    eigen_x=vmem(256, 128), eigen_y=vmem(16, 256), eigen_z=vmem(16, 256), in_sem=DMA((9,)),
    field=vmem(2, 32, 16, 128), rows=vmem(2, 2, 32, 128), ext=vmem(2, 50, YE, 256), row_ext=vmem(2, 2, 16, 256),
    halo_send=DMA((40,)), halo_recv=DMA((40,)),
    root=vmem(2, XE, 48, 128), gain=vmem(2, XE, YE, 128), keep=vmem(2, XE, YE, 128),
    wa=vmem(3, 2, XE, 48, 128), wb=vmem(3, 2, XE, 48, 128), row_w=vmem(2, 2, 4, 16, 128), div=vmem(2, 256, 128), mixed=vmem(256, 256),
    s1=vmem(2, 256, 128), r2=vmem(2, 256, 128), s2=vmem(2, 256, 128), r3=vmem(2, 256, 128), s3=vmem(2, 256, 128),
    r4=vmem(2, 256, 128), s4=vmem(2, 256, 128), r5=vmem(2, 256, 128), lines=vmem(256, 256),
    own_out=vmem(256, 128), peer_out=vmem(256, 128),
    send_sem=DMA((4, 16)), recv_sem=DMA((4, 16)), last_send=DMA(()), last_recv=DMA(()),
)


def whole_kernel(ids_in, class_in, cond_in, first_in, forward_in, cosine_in, eigen_x_in, eigen_y_in, eigen_z_in, table_ref, normals_ref, out_ref, *scratch):
    s = dict(zip(SCRATCH, scratch))
    loads = [pltpu.make_async_copy(src, dst, s["in_sem"].at[k]) for k, (src, dst) in enumerate([
        (ids_in, s["ids"]), (class_in, s["classes"]), (cond_in, s["cond"]), (first_in, s["first"]), (forward_in, s["forward"]), (cosine_in, s["cosine"]),
        (eigen_x_in, s["eigen_x"]), (eigen_y_in, s["eigen_y"]), (eigen_z_in, s["eigen_z"])])]
    barrier = pltpu.get_barrier_semaphore()
    count = greet_halo(barrier)
    for load in loads:
        load.start()
    count += greet_groups(barrier)
    for load in loads[:3]:
        load.wait()
    fill_field(s["ids"], s["classes"], s["cond"], table_ref, s["field"], s["rows"])
    pl.semaphore_wait(barrier, count)
    copies = halo_copies(s["field"], s["rows"], s["ext"], s["row_ext"], s["halo_send"], s["halo_recv"])
    for first, _ in INNER:
        start_all(copies, ("face", first))
    start_all(copies, ("block",), "own", ("row",), ("edge",))
    for first, _ in OUTER:
        start_all(copies, ("face", first))
    for load in loads[3:]:
        load.wait()
    heat_part(normals_ref, copies, s["ext"], s["row_ext"], s["first"], s["s1"], s["root"], s["gain"], s["keep"], s["wa"], s["wb"], s["row_w"], s["div"], s["mixed"])
    solve_part(s["s1"], s["forward"], s["cosine"], s["eigen_x"], s["eigen_y"], s["eigen_z"], out_ref, s["r2"], s["s2"], s["r3"], s["s3"],
               s["r4"], s["s4"], s["r5"], s["lines"], s["own_out"], s["peer_out"], s["mixed"],
               s["send_sem"], s["recv_sem"], s["last_send"], s["last_recv"])


def per_device(surface_ids, class_map, conductivity, normals, class_table):
    cosine = cosine_table()
    eigen = eigen_values()
    cosine_pair, forward_pair = jnp.asarray(halves(cosine)), jnp.asarray(halves(cosine.T.copy()))
    along_z = np.concatenate([np.arange(0, N, 2), np.arange(1, N, 2)])
    first_pair = jnp.asarray(halves(cosine.T[along_z].copy()))
    eigen_x = jnp.asarray(np.repeat(eigen[:, None], 128, axis=1))
    eigen_y = jnp.asarray(np.repeat(eigen.reshape(16, 16), 16, axis=1))
    eigen_z = jnp.asarray(np.tile(eigen.reshape(16, 16), (1, 16)))
    out = pl.pallas_call(
        whole_kernel,
        out_shape=jax.ShapeDtypeStruct((512, 128), f32),
        in_specs=[pl.BlockSpec(memory_space=pltpu.HBM)] * 9 + [SM, VM], out_specs=VM,
        scratch_shapes=list(SCRATCH.values()),
        compiler_params=pltpu.CompilerParams(collective_id=0, has_side_effects=True, vmem_limit_bytes=LIMIT),
    )(surface_ids, class_map, conductivity, first_pair, forward_pair, cosine_pair, eigen_x, eigen_y, eigen_z, class_table, normals)
    return out.reshape(32, 16, 128)


def solution(mesh):
    spec = P("gx", "gy", "gz")
    return jax.shard_map(
        per_device, mesh=mesh, in_specs=(spec, spec, spec, P(), P()), out_specs=spec, check_vma=False
    )
```

time: 83.5 us -> 76.6 us (0.917)
  Pallas kernels: 81.6 us -> 74.8 us
    pallas_call x1, Pallas kernels: 81.6 us -> 74.8 us  [per_device(): pl.pallas_call(whole_kernel, out_shape=jax.ShapeDtypeStruct((512, 128), f...]
where the time goes in v4:
time: 76.6 us; the launch traced here: 76.5 us
  Pallas kernels  74.8 us (98%)
  local copies, waits for them, and re-layouts  1.67 us (2%)
    pallas_call x1, Pallas kernels, per_device(): pl.pallas_call(whole_kernel, out_shape=jax.ShapeDtypeStruct((512, 128), f...  74.8 us
    unnamed x1, local copies, waits for them, and re-layouts  1.67 us

profile of v4, /device:TPU:1, one launch (start us, length us, event | category | flops | bytes accessed | tf_op | source)
XLA Modules:
  0.0 76.5 jit_solution(11851214266344400468)
XLA Ops:
  0.0 74.8 %shard_map.109 = f32[512,128]{1,0:T(8,128)} custom-call(s32[32,16,128]{2,1,0:T(8,128)} %ids_in.1, s32[32,16,128]{2,1,0:T(8,128)} %class_in.1, f32[32,16,128]{2,1,0:T(8,128)} %cond_in.1, bf16[2,256,256]{2,1,0:T(8,128)(2,1)} %constant.14.clone.first_in, bf16[2,256,256]{2,1,0:T(8,128)(2,1)} %constant.13.clone.forward_in, ...), custom_call_target="tpu_custom_call" | custom-call | tf_op jit(solution)/shard_map/pallas_call | solution.py:552
  74.8 1.7 %copy.13 = f32[32,16,128]{2,1,0:T(8,128)} copy(f32[32,16,128]{2,1,0:T(8,128)} %bitcast.1) | data formatting | bytes 524288

commit v5 on v4

--- a/solution.py
+++ b/solution.py
@@ -315,7 +315,11 @@
         for dy in (1, -1):
             copies["face", first, dy].wait()
             copies["pass", first, dy].start()
+    for first, _ in OUTER:
+        start_all(copies, ("face", first))
     looked_up(middle, 12, 25)
+    wait_all(copies, ("edge",))
+    looked_up(middle, 25, XE)
     wait_all(copies, ("row",))
     for side in range(2):
         y = y0 - 9 if side == 0 else y0 + 24
@@ -344,8 +348,7 @@
         elif before == 18:
             wait_all(copies, ("pass", "outer"))
         else:
-            wait_all(copies, ("edge",), ("corner",))
-            looked_up(middle, before, reach)
+            wait_all(copies, ("corner",))
         looked_up(sides, before, reach)
         lax.fori_loop(max(1, before - 1), reach - 1, coefficients, 0, unroll=UNROLL)
         if before == 0:
@@ -399,7 +402,11 @@
     return (index // 2, lax.axis_index("gy"), index % 2)
 
 
-def exchange(src, dst, me, where, send_sem, recv_sem):
+FAR_FIRST_Y = (4, 12, 5, 11, 3, 13, 6, 10, 2, 14, 7, 9, 1, 15, 8)
+FAR_FIRST_X = (12, 4, 11, 13, 3, 5, 10, 14, 2, 6, 8, 7, 9, 1, 15)
+
+
+def exchange(src, dst, me, where, order, send_sem, recv_sem):
     def copy(d):
         to = lax.rem(me + d, 16)
         return pltpu.make_async_remote_copy(
@@ -407,7 +414,7 @@
             dst.at[:, pl.ds(pl.multiple_of(me * 16, 16), 16), :],
             send_sem.at[d], recv_sem.at[d], device_id=where(to), device_id_type=MESH)
 
-    for d in (8, 7, 9, 6, 10, 5, 11, 4, 12, 3, 13, 2, 14, 1, 15):
+    for d in order:
         copy(d).start()
     own = pl.ds(pl.multiple_of(me * 16, 16), 16)
     dst[:, own, :] = src[:, own, :]
@@ -436,11 +443,9 @@
     gx, gy, gz = lax.axis_index("gx"), lax.axis_index("gy"), lax.axis_index("gz")
     group = gx * 2 + gz
 
-    def greet(d, _):
-        pl.semaphore_signal(barrier, inc=1, device_id=y_group(lax.rem(gy + d, 16)), device_id_type=MESH)
-        pl.semaphore_signal(barrier, inc=1, device_id=x_group(lax.rem(group + d, 16)), device_id_type=MESH)
-        return 0
-    lax.fori_loop(1, 16, greet, 0)
+    for dy, dx in zip(FAR_FIRST_Y, FAR_FIRST_X):
+        pl.semaphore_signal(barrier, inc=1, device_id=y_group(lax.rem(gy + dy, 16)), device_id_type=MESH)
+        pl.semaphore_signal(barrier, inc=1, device_id=x_group(lax.rem(group + dx, 16)), device_id_type=MESH)
     return 30
 
 
@@ -450,19 +455,19 @@
     group = gx * 2 + gz
     cosine = (cosine_ref[0], cosine_ref[1])
     forward = (forward_ref[0], forward_ref[1])
-    exchange(s1, r2, gy, y_group, send_sem.at[0], recv_sem.at[0])
+    exchange(s1, r2, gy, y_group, FAR_FIRST_Y, send_sem.at[0], recv_sem.at[0])
     turn(product(cosine, split(whole(r2))), mixed, s2)
-    exchange(s2, r3, group, x_group, send_sem.at[1], recv_sem.at[1])
+    exchange(s2, r3, group, x_group, FAR_FIRST_X, send_sem.at[1], recv_sem.at[1])
     spectrum = product(cosine, split(whole(r3)))
     rest = eigen_y[pl.ds(group, 1), :] + eigen_z[pl.ds(gy, 1), :]
     eigen = jnp.concatenate([eigen_x[...], eigen_x[...]], axis=1)
     solved = -spectrum / (eigen + rest + 4.0 / (N * N))
     turn(product(forward, split(solved)), mixed, s3)
-    exchange(s3, r4, group, x_group, send_sem.at[2], recv_sem.at[2])
+    exchange(s3, r4, group, x_group, FAR_FIRST_X, send_sem.at[2], recv_sem.at[2])
     values = product(forward, split(whole(r4)))
     for h in range(2):
         s4[h] = values[:, h * 128:(h + 1) * 128]
-    exchange(s4, r5, gy, y_group, send_sem.at[3], recv_sem.at[3])
+    exchange(s4, r5, gy, y_group, FAR_FIRST_Y, send_sem.at[3], recv_sem.at[3])
 
     def gather(y, _):
         for xh in range(2):
@@ -471,16 +476,20 @@
                 lines[pl.ds(pl.multiple_of(y * 16 + xh * 8, 8), 8), pl.ds(ah * 128, 128)] = swap8(tile)
         return 0
     lax.fori_loop(0, 16, gather, 0, unroll=SWAP_UNROLL)
-    values = product(split(lines[...]), cosine)
-    first = gz == 0
-    mine = jnp.where(first, values[:, :128], values[:, 128:])
-    theirs = jnp.where(first, values[:, 128:], values[:, :128])
+    pieces = split(lines[...])
+
+    def half_of(core):
+        lanes = pl.ds(pl.multiple_of(core * 128, 128), 128)
+        return product(pieces, (cosine_ref[0, :, lanes], cosine_ref[1, :, lanes]))
+
+    theirs = half_of(1 - gz)
     for y in range(16):
         peer_out[pl.ds(y, 16, stride=16), :] = theirs[y * 16:(y + 1) * 16]
     rows = pl.ds(pl.multiple_of(gz * 256, 256), 256)
     copy = pltpu.make_async_remote_copy(
         peer_out, out_ref.at[rows, :], last_send, last_recv, device_id=(gx, gy, 1 - gz), device_id_type=MESH)
     copy.start()
+    mine = half_of(gz)
     for y in range(16):
         own_out[pl.ds(y, 16, stride=16), :] = mine[y * 16:(y + 1) * 16]
     out_ref[rows, :] = own_out[...]
@@ -518,10 +527,11 @@
         (ids_in, s["ids"]), (class_in, s["classes"]), (cond_in, s["cond"]), (first_in, s["first"]), (forward_in, s["forward"]), (cosine_in, s["cosine"]),
         (eigen_x_in, s["eigen_x"]), (eigen_y_in, s["eigen_y"]), (eigen_z_in, s["eigen_z"])])]
     barrier = pltpu.get_barrier_semaphore()
-    count = greet_halo(barrier)
-    for load in loads:
+    for load in loads[:3]:
         load.start()
-    count += greet_groups(barrier)
+    count = greet_groups(barrier) + greet_halo(barrier)
+    for load in loads[3:]:
+        load.start()
     for load in loads[:3]:
         load.wait()
     fill_field(s["ids"], s["classes"], s["cond"], table_ref, s["field"], s["rows"])
@@ -529,9 +539,7 @@
     copies = halo_copies(s["field"], s["rows"], s["ext"], s["row_ext"], s["halo_send"], s["halo_recv"])
     for first, _ in INNER:
         start_all(copies, ("face", first))
-    start_all(copies, ("block",), "own", ("row",), ("edge",))
-    for first, _ in OUTER:
-        start_all(copies, ("face", first))
+    start_all(copies, "own", ("block",), ("row",), ("edge",))
     for load in loads[3:]:
         load.wait()
     heat_part(normals_ref, copies, s["ext"], s["row_ext"], s["first"], s["s1"], s["root"], s["gain"], s["keep"], s["wa"], s["wb"], s["row_w"], s["div"], s["mixed"])

time: 76.6 us -> 75.4 us (0.984)
  Pallas kernels: 74.8 us -> 73.6 us
    pallas_call x1, Pallas kernels: 74.8 us -> 73.6 us  [per_device(): pl.pallas_call(whole_kernel, out_shape=jax.ShapeDtypeStruct((512, 128), f...]
where the time goes in v5:
time: 75.4 us; the launch traced here: 75.2 us
  Pallas kernels  73.6 us (98%)
  local copies, waits for them, and re-layouts  1.67 us (2%)
    pallas_call x1, Pallas kernels, per_device(): pl.pallas_call(whole_kernel, out_shape=jax.ShapeDtypeStruct((512, 128), f...  73.6 us
    unnamed x1, local copies, waits for them, and re-layouts  1.67 us

profile of v5, /device:TPU:1, one launch (start us, length us, event | category | flops | bytes accessed | tf_op | source)
XLA Modules:
  0.0 75.2 jit_solution(99316361664528873)
XLA Ops:
  0.0 73.6 %shard_map.109 = f32[512,128]{1,0:T(8,128)} custom-call(s32[32,16,128]{2,1,0:T(8,128)} %ids_in.1, s32[32,16,128]{2,1,0:T(8,128)} %class_in.1, f32[32,16,128]{2,1,0:T(8,128)} %cond_in.1, bf16[2,256,256]{2,1,0:T(8,128)(2,1)} %constant.14.clone.first_in, bf16[2,256,256]{2,1,0:T(8,128)(2,1)} %constant.13.clone.forward_in, ...), custom_call_target="tpu_custom_call" | custom-call | tf_op jit(solution)/shard_map/pallas_call | solution.py:560
  73.6 1.7 %copy.13 = f32[32,16,128]{2,1,0:T(8,128)} copy(f32[32,16,128]{2,1,0:T(8,128)} %bitcast.1) | data formatting | bytes 524288

commit v6 on v5

--- a/solution.py
+++ b/solution.py
@@ -352,13 +352,14 @@
         looked_up(sides, before, reach)
         lax.fori_loop(max(1, before - 1), reach - 1, coefficients, 0, unroll=UNROLL)
         if before == 0:
-            for first, _ in OUTER:
-                for dy in (1, -1):
-                    copies["face", first, dy].wait()
-            start_all(copies, ("pass", "outer"), ("corner",))
             for step in range(1, STEPS + 1):
                 src, dst = (wa, wb) if step % 2 else (wb, wa)
                 march(src, dst, step, reach - 2 * step)
+                if step == 2:
+                    for first, _ in OUTER:
+                        for dy in (1, -1):
+                            copies["face", first, dy].wait()
+                    start_all(copies, ("pass", "outer"), ("corner",))
         else:
             def pair(p, _, before=before, reach=reach):
                 for odd, src, dst in ((1, wa, wb), (2, wb, wa)):

time: 75.4 us -> 75.5 us (level)
  no operation moved by 1% of the time
where the time goes in v6:
time: 75.5 us; the launch traced here: 75.4 us
  Pallas kernels  73.7 us (98%)
  local copies, waits for them, and re-layouts  1.67 us (2%)
    pallas_call x1, Pallas kernels, per_device(): pl.pallas_call(whole_kernel, out_shape=jax.ShapeDtypeStruct((512, 128), f...  73.7 us
    unnamed x1, local copies, waits for them, and re-layouts  1.67 us

profile of v6, /device:TPU:1, one launch (start us, length us, event | category | flops | bytes accessed | tf_op | source)
XLA Modules:
  0.0 75.4 jit_solution(1364873966660361271)
XLA Ops:
  0.0 73.7 %shard_map.109 = f32[512,128]{1,0:T(8,128)} custom-call(s32[32,16,128]{2,1,0:T(8,128)} %ids_in.1, s32[32,16,128]{2,1,0:T(8,128)} %class_in.1, f32[32,16,128]{2,1,0:T(8,128)} %cond_in.1, bf16[2,256,256]{2,1,0:T(8,128)(2,1)} %constant.14.clone.first_in, bf16[2,256,256]{2,1,0:T(8,128)(2,1)} %constant.13.clone.forward_in, ...), custom_call_target="tpu_custom_call" | custom-call | tf_op jit(solution)/shard_map/pallas_call | solution.py:561
  73.7 1.7 %copy.13 = f32[32,16,128]{2,1,0:T(8,128)} copy(f32[32,16,128]{2,1,0:T(8,128)} %bitcast.1) | data formatting | bytes 524288
